TPU v7x, 512 devices: a whole 4x4x16 slice. The times are simulated.
512 devices in a mesh: dp: 8 (over y, core), expert: 32 (over z, x_hi), tensor: 2 (over x_lo).
Axes of the slice: x: 4 (x_hi: 2, x_lo: 2; x = x_hi * 2 + x_lo), y: 4, z: 16, core: 2. Of those that a mesh axis runs over, the one named last changes fastest.
Arguments:
- states: bfloat16 [8192, 4096], P(('dp', 'expert'), 'tensor'), parts along dimension 0, may hold values from -512 to 512
- norm_gain: float32 [4096], P('tensor'), may hold values from 0.1 to 1.9
- expert_ids: int32 [8192, 8], P(('dp', 'expert')), parts along dimension 0, may hold values from 0 to 127, as said below
- route_gates: float32 [8192, 8], P(('dp', 'expert')), parts along dimension 0, may hold values from 0.1 to 1
- w_gate: bfloat16 [32, 4096, 384], P('expert', 'tensor'), may hold values from -0.09375 to 0.09375
- w_up: bfloat16 [32, 4096, 384], P('expert', 'tensor'), may hold values from -0.09375 to 0.09375
- w_down: bfloat16 [32, 384, 4096], P('expert', None, 'tensor'), may hold values from -0.15625 to 0.15625
Outputs:
- mixture: bfloat16 [8192, 4096], P(('dp', 'expert'), 'tensor'), parts along dimension 0
There are 8 independent parts, one for each index of `dp`. A program takes and returns all parts, laid end to end along the dimension named above; an argument that names none is the same for every part. Nothing has to cross between parts.
Inputs may be any that keep to these rules, and one draw needn't show every extreme that they name: `expert_ids`: each row names 8 different experts. Among the 32 rows of one index of expert (aligned blocks), each expert below 8 is named by at most 16 rows, and in every draw some expert below 8 is named by exactly 16 rows in every block.
All inputs are finite; a program needn't handle non-finite values.
Results may differ from a plain program's by a relative error of at most 0.014.
Values may be sent and summed in bfloat16 or wider, within the bound.
No kernel may reach another device: no remote copies, remote signals or barrier semaphores. Data moves between devices by JAX's collectives and lax.ppermute only.
A program may use at most 64 MiB of HBM per device.

v0:
```python
import jax
import jax.numpy as jnp
from jax import lax
from jax.sharding import PartitionSpec as P

D = 4096
GROUP = 4


EPSILON = 1e-06


def shards(states, norm_gain, expert_ids, route_gates, w_gate, w_up, w_down):
    tokens_here = states.shape[0]
    width_here = states.shape[1]
    devices = lax.axis_size("expert")
    flights = devices // GROUP
    capacity = tokens_here // 2
    values = states.astype(jnp.float32)
    squares = lax.psum(jnp.sum(values * values, axis=1), "tensor")
    scaling = lax.rsqrt(squares / D + EPSILON)
    normed = (values * scaling[:, None] * norm_gain[None, :]).astype(jnp.bfloat16)
    flight_ids = jnp.arange(flights, dtype=jnp.int32)
    matches = expert_ids[:, :, None] == flight_ids[None, None, :]
    member = jnp.any(matches, axis=1)
    weight = jnp.sum(jnp.where(matches, route_gates[:, :, None], 0.0), axis=1)
    position = jnp.cumsum(member.astype(jnp.int32), axis=0) - 1
    slot_ids = jnp.arange(capacity, dtype=jnp.int32)
    placed = (position.T[:, None, :] == slot_ids[None, :, None]) & member.T[:, None, :]
    packed = jnp.einsum(
        "fct,td->fcd", placed.astype(jnp.bfloat16), normed, preferred_element_type=jnp.float32
    ).astype(jnp.bfloat16)
    outgoing = jnp.repeat(packed, GROUP, axis=0)
    arrived = lax.all_to_all(outgoing, "expert", split_axis=0, concat_axis=0, tiled=True)
    received_rows = arrived.reshape(devices * capacity, width_here)
    gate_part = jnp.dot(received_rows, w_gate[0], preferred_element_type=jnp.float32)
    up_part = jnp.dot(received_rows, w_up[0], preferred_element_type=jnp.float32)
    gate_sum, up_sum = lax.psum((gate_part, up_part), "tensor")
    hidden = (jax.nn.silu(gate_sum) * up_sum).astype(jnp.bfloat16)
    partial_value = jnp.dot(hidden, w_down[0], preferred_element_type=jnp.float32)
    returned = lax.all_to_all(
        partial_value.reshape(devices, capacity, width_here).astype(jnp.bfloat16),
        "expert",
        split_axis=0,
        concat_axis=0,
        tiled=True,
    ).astype(jnp.float32)
    expert_out = jnp.sum(returned.reshape(flights, GROUP, capacity, width_here), axis=1).astype(
        jnp.bfloat16
    )
    weighted = placed.astype(jnp.float32) * weight.T[:, None, :]
    mixture = jnp.einsum(
        "fct,fcd->td", weighted, expert_out.astype(jnp.float32), precision=lax.Precision.HIGHEST
    )
    return mixture.astype(jnp.bfloat16)


def solution(mesh):
    return jax.shard_map(
        shards,
        mesh=mesh,
        in_specs=(
            P(("dp", "expert"), "tensor"),
            P("tensor"),
            P(("dp", "expert"), None),
            P(("dp", "expert"), None),
            P("expert", "tensor", None),
            P("expert", "tensor", None),
            P("expert", None, "tensor"),
        ),
        out_specs=P(("dp", "expert"), "tensor"),
        check_vma=False,
    )
```

profile of v0, /device:TPU:4, one launch (start us, length us, event | category | flops | bytes accessed | tf_op | source)
XLA Modules:
  0.0 330.3 jit_solution(6085957511569286183)
XLA Ops:
  6.5 0.0 copy-start
  6.5 0.0 all-reduce.3.cloned.1.call-start
  6.5 0.8 fusion.21
  7.4 0.1 copy.12
  7.4 0.1 reduce_window_sum.11
  7.5 0.1 copy.13
  7.6 1.0 fusion.6
  8.6 4.9 %psum.21 = f32[32]{0:T(128)S(1)} all-reduce(f32[32]{0:T(128)S(1)} %fusion.6), channel_id=1, replica_groups=mesh['dp'=8,'expert'=32,'tensor'=2] {'tensor'}, use_global_device_ids=true, to_apply=%region_4.5 | all-reduce | flops 32 | bytes 256 | tf_op jit(solution)/shard_map/psum | solution.py:20
  13.6 1.3 convolution_convert_fusion.1
  14.8 0.2 broadcast_in_dim.16
  15.1 0.0 copy-start.3
  15.1 116.6 %all_to_all.10 = bf16[32,16,2048]{2,1,0:T(8,128)(2,1)S(1)} all-to-all(bf16[32,16,2048]{2,1,0:T(8,128)(2,1)S(1)} %bitcast.30), channel_id=1, replica_groups=mesh['dp'=8,'expert'=32,'tensor'=2] {'expert'}, dimensions={0} | all-to-all | bytes 4194304 | tf_op jit(solution)/shard_map/all_to_all | solution.py:34
  131.7 0.0 copy-done.3
  131.7 0.0 copy-start.4
  131.7 2.1 fusion.2
  133.9 0.0 copy-done.4
  133.9 2.1 fusion.4
  136.0 0.0 all-reduce.3.cloned.1.call-update
  136.0 65.4 %all-reduce.3.cloned.1.call-done = (f32[512,384]{1,0:T(8,128)}, f32[512,384]{1,0:T(8,128)}) async-done(((f32[512,384]{1,0:T(8,128)}, f32[512,384]{1,0:T(8,128)}), (f32[512,384]{1,0:T(8,128)}, f32[512,384]{1,0:T(8,128)})) %all-reduce.3.cloned.1.call-update) | async-done | bytes 1572880 | tf_op jit(solution)/shard_map/psum | solution.py:38
  201.5 1.6 multiply_convert_fusion
  203.1 0.0 copy-done
  203.1 2.6 convolution_convert_fusion
  205.7 0.0 copy-start.1
  205.7 0.0 copy-start.2
  205.7 15.5 %all-to-all-start.1 = ((bf16[32,16,2048]{2,1,0:T(8,128)(2,1)}), bf16[32,16,2048]{2,1,0:T(8,128)(2,1)}, u32[]{:S(2)}, u32[]{:S(2)}) async-start(bf16[32,16,2048]{2,1,0:T(8,128)(2,1)} %convolution_convert_fusion), calls=%async_computation.1 | async-start | bytes 4194304 | tf_op jit(solution)/shard_map/all_to_all | solution.py:41
  221.2 0.0 copy-done.1
  221.2 0.0 copy-done.2
  221.2 99.3 %all-to-all-done.1 = bf16[32,16,2048]{2,1,0:T(8,128)(2,1)} async-done(((bf16[32,16,2048]{2,1,0:T(8,128)(2,1)}), bf16[32,16,2048]{2,1,0:T(8,128)(2,1)}, u32[]{:S(2)}, u32[]{:S(2)}) %all-to-all-start.1) | async-done | bytes 2097184 | tf_op jit(solution)/shard_map/all_to_all | solution.py:41
  320.5 2.0 bitcast_reduce_fusion
  322.4 1.1 fusion
  (4 shorter events, 0.0 us)
Async XLA Ops:
  6.5 196.5 %copy-start = (bf16[1,384,2048]{2,1,0:T(8,128)(2,1)S(1)}, bf16[1,384,2048]{2,1,0:T(8,128)(2,1)}, u32[]{:S(2)}) copy-start(bf16[1,384,2048]{2,1,0:T(8,128)(2,1)} %param.13) | copy-start | bytes 4718596
  6.5 194.9 %all-reduce.3.cloned.1.call-start = ((), (), s32[]{:S(2)}) async-start(), calls=%async_computation.2 | async-start | bytes 3145728 | tf_op jit(solution)/shard_map/psum | solution.py:38
  15.1 116.6 %copy-start.3 = (bf16[1,2048,384]{2,1,0:T(8,128)(2,1)S(1)}, bf16[1,2048,384]{2,1,0:T(8,128)(2,1)}, u32[]{:S(2)}) copy-start(bf16[1,2048,384]{2,1,0:T(8,128)(2,1)} %param.12) | copy-start | bytes 4718596
  131.7 2.1 copy-start.4
  205.7 15.5 %copy-start.1 = (s32[32,8]{0,1:T(8,128)S(1)}, s32[32,8]{0,1:T(8,128)}, u32[]{:S(2)}) copy-start(s32[32,8]{0,1:T(8,128)} %param.9) | copy-start | bytes 3076
  205.7 15.5 %copy-start.2 = (f32[32,8]{0,1:T(8,128)S(1)}, f32[32,8]{0,1:T(8,128)}, u32[]{:S(2)}) copy-start(f32[32,8]{0,1:T(8,128)} %param.10) | copy-start | bytes 3076
  205.7 114.8 %all-to-all-start.1 = ((bf16[32,16,2048]{2,1,0:T(8,128)(2,1)}), bf16[32,16,2048]{2,1,0:T(8,128)(2,1)}, u32[]{:S(2)}, u32[]{:S(2)}) async-start(bf16[32,16,2048]{2,1,0:T(8,128)(2,1)} %convolution_convert_fusion), calls=%async_computation.1 | async-start | bytes 4194304 | tf_op jit(solution)/shard_map/all_to_all | solution.py:41
Sparse Core Ops, SparseCore 0:
  136.2 65.2 all-reduce.2
where the time goes:
time: 331 us; the launch traced here: 330 us
  waiting for transfers between devices  165 us (50%)
  blocking collectives  122 us (37%)
  starting transfers between devices  15.5 us (5%)
  between operations  13.5 us (4%)
  matrix products  9.17 us (3%)
  other arithmetic  5.51 us (2%)
    all_to_all x1, blocking collectives, shards(): lax.all_to_all(outgoing, 'expert', split_axis=0, concat_axis=0, tiled=True)  117 us
    all_to_all x1, waiting for transfers between devices, shards(): lax.all_to_all(partial_value.reshape(devices, capacity, width_here).astyp...  99.3 us
    psum x1, waiting for transfers between devices, shards(): gate_sum, up_sum = lax.psum((gate_part, up_part), 'tensor')  65.4 us
    all_to_all x1, starting transfers between devices, shards(): lax.all_to_all(partial_value.reshape(devices, capacity, width_here).astyp...  15.5 us
  transfers between devices with their start and end apart: 2, of which 2 were waited for; matrix products, arithmetic and copies ran while one was open for 0% of the time, Pallas kernels for 0%

commit v1 on v0

v1 whole, which is shorter than its diff:
```python
import jax
import jax.numpy as jnp
from jax import lax
from jax.sharding import Mesh, PartitionSpec as P

D = 4096
GROUP = 4
EPSILON = 1e-06
SWAP = [(0, 1), (1, 0)]


def shards(states, norm_gain, expert_ids, route_gates, w_gate, w_up, w_down):
    tokens, width = states.shape
    units = w_gate.shape[2]
    depth = lax.axis_size("z")
    replicas = lax.axis_size("y") * lax.axis_size("core")
    experts = depth * lax.axis_size("xh") // GROUP
    spread = depth // experts
    capacity = tokens // 2
    rows = depth * capacity

    replica = lax.axis_index("y") * lax.axis_size("core") + lax.axis_index("core")
    share, down_share = width // replicas, units // replicas
    mine = jnp.concatenate(
        [
            lax.dynamic_slice_in_dim(w_gate[0], replica * share, share, 0),
            lax.dynamic_slice_in_dim(w_up[0], replica * share, share, 0),
        ],
        axis=1,
    )
    mine_down = lax.dynamic_slice_in_dim(w_down[0], replica * down_share, down_share, 0)
    other = lax.ppermute(mine, "xh", SWAP)
    other_down = lax.ppermute(mine_down, "xh", SWAP)
    w_in_other = lax.all_gather(other, ("y", "core"), axis=0, tiled=True)
    w_down_other = lax.all_gather(other_down, ("y", "core"), axis=0, tiled=True)

    flight_ids = jnp.arange(experts, dtype=jnp.int32)
    matches = expert_ids[:, :, None] == flight_ids[None, None, :]
    member = jnp.any(matches, axis=1)
    weight = jnp.sum(jnp.where(matches, route_gates[:, :, None], 0.0), axis=1)
    before = jnp.tril(jnp.ones((tokens, tokens), jnp.float32), -1)
    position = jnp.dot(before, member.astype(jnp.float32)).astype(jnp.int32)
    slots = jnp.where(member, position, capacity)
    slots = jnp.repeat(slots, spread, axis=1)
    slot_ids = jnp.arange(capacity, dtype=jnp.int32)
    placed = slots.T[:, None, :] == slot_ids[None, :, None]
    placed = placed.reshape(rows, tokens)
    packed = jnp.dot(
        placed.astype(jnp.bfloat16), states, preferred_element_type=jnp.float32
    ).astype(jnp.bfloat16)
    arrived = lax.all_to_all(
        packed.reshape(depth, capacity, width), "z", split_axis=0, concat_axis=0, tiled=True
    ).reshape(rows, width)

    values = arrived.astype(jnp.float32)
    squares = jnp.sum(values * values, axis=1, keepdims=True)
    scaled = (values * norm_gain[None, :]).astype(jnp.bfloat16)

    def dot(a, b):
        return jnp.dot(a, b, preferred_element_type=jnp.float32)

    part_other = dot(scaled, w_in_other)
    part = jnp.concatenate(
        [dot(scaled, w_gate[0]), dot(scaled, w_up[0]), part_other], axis=1
    )
    total = part + lax.ppermute(part.astype(jnp.bfloat16), "xl", SWAP).astype(jnp.float32)
    squares = squares + lax.ppermute(squares, "xl", SWAP)
    total = total * lax.rsqrt(squares / D + EPSILON)
    total = total.reshape(rows, 2, 2, units)
    hidden = (jax.nn.silu(total[:, :, 0]) * total[:, :, 1]).astype(jnp.bfloat16)
    partial_value = dot(hidden[:, 0], w_down[0]) + dot(hidden[:, 1], w_down_other)
    returned = lax.all_to_all(
        partial_value.astype(jnp.bfloat16).reshape(depth, capacity, width),
        "z",
        split_axis=0,
        concat_axis=0,
        tiled=True,
    ).reshape(rows, width)

    wide = jnp.repeat(weight, spread, axis=1).T
    weighted = jnp.where(placed, jnp.repeat(wide, capacity, axis=0), 0.0)
    high = weighted.astype(jnp.bfloat16)
    low = (weighted - high.astype(jnp.float32)).astype(jnp.bfloat16)
    both = lax.dot_general(
        jnp.concatenate([high, low], axis=1),
        returned,
        (((0,), (0,)), ((), ())),
        preferred_element_type=jnp.float32,
    )
    return (both[:tokens] + both[tokens:]).astype(jnp.bfloat16)


def solution(mesh):
    x_hi = 2
    dp, expert, tensor = (mesh.shape[name] for name in ("dp", "expert", "tensor"))
    fine = Mesh(
        mesh.devices.reshape(dp // 2, 2, expert // x_hi, x_hi, tensor),
        ("y", "core", "z", "xh", "xl"),
    )
    tokens, slices = ("y", "core", "z", "xh"), ("z", "xh")
    return jax.shard_map(
        shards,
        mesh=fine,
        in_specs=(
            P(tokens, "xl"),
            P("xl"),
            P(tokens, None),
            P(tokens, None),
            P(slices, "xl", None),
            P(slices, "xl", None),
            P(slices, None, "xl"),
        ),
        out_specs=P(tokens, "xl"),
        check_vma=False,
    )
```

time: 331 us -> 200 us (0.60)
  blocking collectives: 122 us -> 0 us
  waiting for transfers between devices: 165 us -> 112 us
  starting transfers between devices: 15.5 us -> 45.4 us
  local copies, waits for them, and re-layouts: 0.41 us -> 10.5 us
    all_to_all x1 -> x0, blocking collectives: 117 us -> none  [shards(): lax.all_to_all(outgoing, 'expert', split_axis=0, concat_axis=0, tiled=True)]
    psum x1 -> x0, waiting for transfers between devices: 65.4 us -> none  [shards(): gate_sum, up_sum = lax.psum((gate_part, up_part), 'tensor')]
    ppermute x0 -> x4, waiting for transfers between devices: none -> 22.9 us  [the longest x1 9.79 us: shards(): squares = squares + lax.ppermute(squares, 'xl', SWAP)]
    ppermute x0 -> x4, starting transfers between devices: none -> 16 us  [the longest x1 7.79 us: shards(): other = lax.ppermute(mine, 'xh', SWAP)]
    all_to_all x1 -> x2, starting transfers between devices: 15.5 us -> 29.3 us  [the longest x1 15.3 us: shards(): lax.all_to_all(packed.reshape(depth, capacity, width), 'z', split_axis=0,...]
    all_to_all x1 -> x2, waiting for transfers between devices: 99.3 us -> 88.6 us  [the longest x1 49.3 us: shards(): lax.all_to_all(partial_value.astype(jnp.bfloat16).reshape(depth, capacity...]
    psum x1 -> x0, blocking collectives: 4.94 us -> none  [shards(): squares = lax.psum(jnp.sum(values * values, axis=1), 'tensor')]
    unnamed x10 -> x30, local copies, waits for them, and re-layouts: 0.02 us -> 3.44 us
  transfers between devices with their start and end apart: 2 -> 8, of which waited for: 2 -> 5; matrix products, arithmetic and copies ran while one was open for 0% -> 10% of each run, Pallas kernels for 0% -> 0%
where the time goes in v1:
time: 200 us; the launch traced here: 199 us
  waiting for transfers between devices  112 us (56%)
  starting transfers between devices  45.4 us (23%)
  between operations  13.7 us (7%)
  matrix products  12.4 us (6%)
  local copies, waits for them, and re-layouts  10.5 us (5%)
  other arithmetic  5.95 us (3%)
    all_to_all x1, waiting for transfers between devices, shards(): lax.all_to_all(partial_value.astype(jnp.bfloat16).reshape(depth, capacity...  49.3 us
    all_to_all x1, waiting for transfers between devices, shards(): lax.all_to_all(packed.reshape(depth, capacity, width), 'z', split_axis=0,...  39.3 us
    all_to_all x1, starting transfers between devices, shards(): lax.all_to_all(packed.reshape(depth, capacity, width), 'z', split_axis=0,...  15.3 us
    all_to_all x1, starting transfers between devices, shards(): lax.all_to_all(partial_value.astype(jnp.bfloat16).reshape(depth, capacity...  14 us
    dot_general x5, matrix products, dot(): return jnp.dot(a, b, preferred_element_type=jnp.float32)  10.5 us
    ppermute x1, waiting for transfers between devices, shards(): squares = squares + lax.ppermute(squares, 'xl', SWAP)  9.79 us
    ppermute x1, starting transfers between devices, shards(): other = lax.ppermute(mine, 'xh', SWAP)  7.79 us
    ppermute x1, waiting for transfers between devices, shards(): other_down = lax.ppermute(mine_down, 'xh', SWAP)  6.65 us
  transfers between devices with their start and end apart: 8, of which 5 were waited for; matrix products, arithmetic and copies ran while one was open for 10% of the time, Pallas kernels for 0%

profile of v1, /device:TPU:4, one launch (start us, length us, event | category | flops | bytes accessed | tf_op | source)
XLA Modules:
  0.0 199.5 jit_solution(12768215594530210829)
XLA Ops:
  6.6 1.2 dynamic-slice_bitcast_fusion.1
  7.8 7.8 %collective-permute-start = (bf16[256,768]{1,0:T(8,128)(2,1)S(1)}, bf16[256,768]{1,0:T(8,128)(2,1)S(1)}, u32[]{:S(2)}, u32[]{:S(2)}) collective-permute-start(bf16[256,768]{1,0:T(8,128)(2,1)S(1)} %pad_maximum_fusion.1), channel_id=1, source_target_pairs={{0,2},{2,0},{1,3},{3,1},{4,6},{6,4},{5,7},{7,5},{8,10},{10,8},{9,1... | collective-permute-start | bytes 1179656 | tf_op jit(solution)/shard_map/ppermute | solution.py:32
  15.6 6.5 %collective-permute-done = bf16[256,768]{1,0:T(8,128)(2,1)S(1)} collective-permute-done((bf16[256,768]{1,0:T(8,128)(2,1)S(1)}, bf16[256,768]{1,0:T(8,128)(2,1)S(1)}, u32[]{:S(2)}, u32[]{:S(2)}) %collective-permute-start) | collective-permute-done | bytes 393248 | tf_op jit(solution)/shard_map/ppermute | solution.py:32
  22.1 0.8 copy-done.6
  23.4 0.6 select_convert_fusion
  24.0 1.5 convolution_convert_fusion
  25.5 15.3 %all-to-all-start = ((bf16[16,16,2048]{2,1,0:T(8,128)(2,1)}), bf16[16,16,2048]{2,1,0:T(8,128)(2,1)S(1)}, u32[]{:S(2)}, u32[]{:S(2)}) async-start(bf16[16,16,2048]{2,1,0:T(8,128)(2,1)} %bitcast.59), calls=%async_computation | async-start | bytes 2097152 | tf_op jit(solution)/shard_map/all_to_all | solution.py:51
  40.9 2.4 %collective-permute-start.3 = (bf16[48,2048]{1,0:T(8,128)(2,1)S(1)}, bf16[48,2048]{1,0:T(8,128)(2,1)S(1)}, u32[]{:S(2)}, u32[]{:S(2)}) collective-permute-start(bf16[48,2048]{1,0:T(8,128)(2,1)S(1)} %dynamic-slice_bitcast_fusion), channel_id=1, source_target_pairs={{0,2},{2,0},{1,3},{3,1},{4,6},{6,4},{5,7},{7,5},{8,10},{10,8},{9,1... | collective-permute-start | bytes 589832 | tf_op jit(solution)/shard_map/ppermute | solution.py:33
  43.4 6.6 %collective-permute-done.3 = bf16[48,2048]{1,0:T(8,128)(2,1)S(1)} collective-permute-done((bf16[48,2048]{1,0:T(8,128)(2,1)S(1)}, bf16[48,2048]{1,0:T(8,128)(2,1)S(1)}, u32[]{:S(2)}, u32[]{:S(2)}) %collective-permute-start.3) | collective-permute-done | bytes 196640 | tf_op jit(solution)/shard_map/ppermute | solution.py:33
  50.0 0.7 copy-done.9
  50.7 39.3 %all-to-all-done = bf16[16,16,2048]{2,1,0:T(8,128)(2,1)S(1)} async-done(((bf16[16,16,2048]{2,1,0:T(8,128)(2,1)}), bf16[16,16,2048]{2,1,0:T(8,128)(2,1)S(1)}, u32[]{:S(2)}, u32[]{:S(2)}) %all-to-all-start) | async-done | bytes 1048608 | tf_op jit(solution)/shard_map/all_to_all | solution.py:51
  90.0 0.4 multiply_reduce_fusion
  90.4 1.0 copy-done.3
  91.4 0.7 fusion.4
  92.1 0.7 fusion.6
  92.9 1.2 fusion.1
  94.1 3.2 %fusion.26 = f32[256,768]{1,0:T(8,128)S(1)} fusion(bf16[256,2048]{1,0:T(8,128)(2,1)} %fusion.1, bf16[2048,768]{1,0:T(8,128)(2,1)} %all-gather.3.cloned.1.call-done), kind=kOutput, calls=%fused_computation.51 | convolution fusion | flops 805306368 | bytes 4980736 | tf_op jit(solution)/shard_map/dot_general | solution.py:60
  97.3 1.1 fusion.8
  98.4 3.1 %collective-permute-start.1 = (bf16[256,1536]{1,0:T(8,128)(2,1)}, bf16[256,1536]{1,0:T(8,128)(2,1)S(1)}, u32[]{:S(2)}, u32[]{:S(2)}) collective-permute-start(bf16[256,1536]{1,0:T(8,128)(2,1)} %fusion.8), channel_id=1, source_target_pairs={{0,1},{1,0},{2,3},{3,2},{4,5},{5,4},{6,7},{7,6},{8,9},{9,8},{10,11... | collective-permute-start | bytes 2359304 | tf_op jit(solution)/shard_map/ppermute | solution.py:66
  101.6 2.7 %collective-permute-start.2 = (f32[256,1]{0,1:T(1,128)S(1)}, f32[256,1]{0,1:T(1,128)S(1)}, u32[]{:S(2)}, u32[]{:S(2)}) collective-permute-start(f32[256,1]{0,1:T(1,128)S(1)} %broadcast_in_dim.54), channel_id=1, source_target_pairs={{0,1},{1,0},{2,3},{3,2},{4,5},{5,4},{6,7},{7,6},{8,9},{9,8},{10,11... | collective-permute-start | bytes 3080 | tf_op jit(solution)/shard_map/ppermute | solution.py:67
  104.3 9.8 %collective-permute-done.2 = f32[256,1]{0,1:T(1,128)S(1)} collective-permute-done((f32[256,1]{0,1:T(1,128)S(1)}, f32[256,1]{0,1:T(1,128)S(1)}, u32[]{:S(2)}, u32[]{:S(2)}) %collective-permute-start.2) | collective-permute-done | bytes 1056 | tf_op jit(solution)/shard_map/ppermute | solution.py:67
  114.1 0.9 copy-done.5
  115.1 1.7 add_multiply_fusion
  116.7 2.2 %reshape.51 = f32[256,2,2,384]{3,2,1,0:T(2,128)} reshape(f32[256,1536]{1,0:T(8,128)S(1)} %add_multiply_fusion) | data formatting | bytes 3145728 | tf_op jit(solution)/shard_map/reshape | solution.py:69
  118.9 3.3 %fusion.25 = (f32[256,2,1,384]{3,2,1,0:T(1,128)S(1)}, f32[256,2,1,384]{3,2,1,0:T(1,128)S(1)}) fusion(f32[256,2,2,384]{3,2,1,0:T(2,128)} %reshape.51), kind=kLoop, calls=%fused_computation.50 | loop fusion | bytes 3145728 | tf_op jit(solution)/shard_map/slice | solution.py:70
  122.2 0.2 fusion.11
  122.5 2.1 %fusion.2 = f32[256,2048]{1,0:T(8,128)} fusion(bf16[1,384,2048]{2,1,0:T(8,128)(2,1)S(1)} %copy-done, bf16[256,2,384]{2,0,1:T(8,128)(2,1)S(1)} %fusion.11), kind=kOutput, calls=%fused_computation.8 | convolution fusion | flops 402653184 | bytes 3866624 | tf_op jit(solution)/shard_map/dot_general | solution.py:60
  124.5 3.8 %fusion = bf16[256,2048]{1,0:T(8,128)(2,1)} fusion(f32[256,2048]{1,0:T(8,128)} %fusion.2, bf16[384,2048]{1,0:T(8,128)(2,1)} %all-gather.5.cloned.1.call-done, bf16[256,2,384]{2,0,1:T(8,128)(2,1)S(1)} %fusion.11), kind=kOutput, calls=%fused_computation.1 | convolution fusion | flops 403701760 | bytes 4915200 | tf_op jit(solution)/shard_map/dot_general | solution.py:60
  128.3 14.0 %all-to-all-start.1 = ((bf16[16,16,2048]{2,1,0:T(8,128)(2,1)}), bf16[16,16,2048]{2,1,0:T(8,128)(2,1)S(1)}, u32[]{:S(2)}, u32[]{:S(2)}) async-start(bf16[16,16,2048]{2,1,0:T(8,128)(2,1)} %bitcast.20), calls=%async_computation.1 | async-start | bytes 2097152 | tf_op jit(solution)/shard_map/all_to_all | solution.py:72
  142.3 49.3 %all-to-all-done.1 = bf16[16,16,2048]{2,1,0:T(8,128)(2,1)S(1)} async-done(((bf16[16,16,2048]{2,1,0:T(8,128)(2,1)}), bf16[16,16,2048]{2,1,0:T(8,128)(2,1)S(1)}, u32[]{:S(2)}, u32[]{:S(2)}) %all-to-all-start.1) | async-done | bytes 1048608 | tf_op jit(solution)/shard_map/all_to_all | solution.py:72
  191.6 0.3 fusion.13
  191.9 0.7 fusion.12
  (50 shorter events, 0.8 us)
Async XLA Ops:
  6.5 34.4 %copy-start = (bf16[1,384,2048]{2,1,0:T(8,128)(2,1)S(1)}, bf16[1,384,2048]{2,1,0:T(8,128)(2,1)}, u32[]{:S(2)}) copy-start(bf16[1,384,2048]{2,1,0:T(8,128)(2,1)} %param.13) | copy-start | bytes 4718596
  6.5 16.3 %copy-start.14 = (f32[32,8]{0,1:T(8,128)S(1)}, f32[32,8]{0,1:T(8,128)}, u32[]{:S(2)}) copy-start(f32[32,8]{0,1:T(8,128)} %param.10) | copy-start | bytes 3076
  6.5 16.3 %copy-start.13 = (s32[32,8]{0,1:T(8,128)S(1)}, s32[32,8]{0,1:T(8,128)}, u32[]{:S(2)}) copy-start(s32[32,8]{0,1:T(8,128)} %param.9) | copy-start | bytes 3076
  6.5 17.5 %copy-start.10 = (bf16[32,2048]{1,0:T(8,128)(2,1)S(1)}, bf16[32,2048]{1,0:T(8,128)(2,1)}, u32[]{:S(2)}) copy-start(bf16[32,2048]{1,0:T(8,128)(2,1)} %param.7) | copy-start | bytes 393220
  6.5 87.6 %all-gather.3.cloned.1.call-start = ((), (), s32[]{:S(2)}) async-start(), calls=%async_computation.2 | async-start | bytes 3538944 | tf_op jit(solution)/shard_map/all_gather | solution.py:34
  7.8 14.3 %collective-permute-start = (bf16[256,768]{1,0:T(8,128)(2,1)S(1)}, bf16[256,768]{1,0:T(8,128)(2,1)S(1)}, u32[]{:S(2)}, u32[]{:S(2)}) collective-permute-start(bf16[256,768]{1,0:T(8,128)(2,1)S(1)} %pad_maximum_fusion.1), channel_id=1, source_target_pairs={{0,2},{2,0},{1,3},{3,1},{4,6},{6,4},{5,7},{7,5},{8,10},{10,8},{9,1... | collective-permute-start | bytes 1179656 | tf_op jit(solution)/shard_map/ppermute | solution.py:32
  22.1 0.8 copy-start.6
  23.0 2.5 %copy-start.7 = (f32[256,32]{0,1:T(8,128)}, f32[256,32]{0,1:T(8,128)S(1)}, u32[]{:S(2)}) copy-start(f32[256,32]{0,1:T(8,128)S(1)} %copy.24) | copy-start | bytes 98308
  25.5 64.5 %copy-start.12 = (f32[2048]{0:T(1024)S(1)}, f32[2048]{0:T(1024)}, u32[]{:S(2)}) copy-start(f32[2048]{0:T(1024)} %param.8) | copy-start | bytes 24580
  25.5 64.5 %all-to-all-start = ((bf16[16,16,2048]{2,1,0:T(8,128)(2,1)}), bf16[16,16,2048]{2,1,0:T(8,128)(2,1)S(1)}, u32[]{:S(2)}, u32[]{:S(2)}) async-start(bf16[16,16,2048]{2,1,0:T(8,128)(2,1)} %bitcast.59), calls=%async_computation | async-start | bytes 2097152 | tf_op jit(solution)/shard_map/all_to_all | solution.py:51
  40.8 83.7 %all-gather.5.cloned.1.call-start = ((), (), s32[]{:S(2)}) async-start(), calls=%async_computation.3 | async-start | bytes 1769472 | tf_op jit(solution)/shard_map/all_gather | solution.py:35
  40.9 9.1 %collective-permute-start.3 = (bf16[48,2048]{1,0:T(8,128)(2,1)S(1)}, bf16[48,2048]{1,0:T(8,128)(2,1)S(1)}, u32[]{:S(2)}, u32[]{:S(2)}) collective-permute-start(bf16[48,2048]{1,0:T(8,128)(2,1)S(1)} %dynamic-slice_bitcast_fusion), channel_id=1, source_target_pairs={{0,2},{2,0},{1,3},{3,1},{4,6},{6,4},{5,7},{7,5},{8,10},{10,8},{9,1... | collective-permute-start | bytes 589832 | tf_op jit(solution)/shard_map/ppermute | solution.py:33
  50.0 0.7 copy-start.9
  90.0 1.4 copy-start.3
  90.4 1.8 copy-start.4
  92.9 5.5 %copy-start.1 = (f32[256,384]{1,0:T(8,128)}, f32[256,384]{1,0:T(8,128)S(1)}, u32[]{:S(2)}) copy-start(f32[256,384]{1,0:T(8,128)S(1)} %fusion.6) | copy-start | bytes 1179652
  97.3 4.2 %copy-start.2 = (f32[256,768]{1,0:T(8,128)}, f32[256,768]{1,0:T(8,128)S(1)}, u32[]{:S(2)}) copy-start(f32[256,768]{1,0:T(8,128)S(1)} %fusion.26) | copy-start | bytes 2359300
  98.4 15.7 %collective-permute-start.1 = (bf16[256,1536]{1,0:T(8,128)(2,1)}, bf16[256,1536]{1,0:T(8,128)(2,1)S(1)}, u32[]{:S(2)}, u32[]{:S(2)}) collective-permute-start(bf16[256,1536]{1,0:T(8,128)(2,1)} %fusion.8), channel_id=1, source_target_pairs={{0,1},{1,0},{2,3},{3,2},{4,5},{5,4},{6,7},{7,6},{8,9},{9,8},{10,11... | collective-permute-start | bytes 2359304 | tf_op jit(solution)/shard_map/ppermute | solution.py:66
  101.6 12.5 %collective-permute-start.2 = (f32[256,1]{0,1:T(1,128)S(1)}, f32[256,1]{0,1:T(1,128)S(1)}, u32[]{:S(2)}, u32[]{:S(2)}) collective-permute-start(f32[256,1]{0,1:T(1,128)S(1)} %broadcast_in_dim.54), channel_id=1, source_target_pairs={{0,1},{1,0},{2,3},{3,2},{4,5},{5,4},{6,7},{7,6},{8,9},{9,8},{10,11... | collective-permute-start | bytes 3080 | tf_op jit(solution)/shard_map/ppermute | solution.py:67
  114.1 0.9 copy-start.5
  128.3 14.0 %copy-start.8 = (f32[256,32]{0,1:T(8,128)S(1)}, f32[256,32]{0,1:T(8,128)}, u32[]{:S(2)}) copy-start(f32[256,32]{0,1:T(8,128)} %copy-done.7) | copy-start | bytes 98308
  128.3 63.3 %copy-start.11 = (bf16[256,32]{0,1:T(8,128)(2,1)S(1)}, bf16[256,32]{0,1:T(8,128)(2,1)}, u32[]{:S(2)}) copy-start(bf16[256,32]{0,1:T(8,128)(2,1)} %get-tuple-element.5) | copy-start | bytes 49156
  128.3 63.3 %all-to-all-start.1 = ((bf16[16,16,2048]{2,1,0:T(8,128)(2,1)}), bf16[16,16,2048]{2,1,0:T(8,128)(2,1)S(1)}, u32[]{:S(2)}, u32[]{:S(2)}) async-start(bf16[16,16,2048]{2,1,0:T(8,128)(2,1)} %bitcast.20), calls=%async_computation.1 | async-start | bytes 2097152 | tf_op jit(solution)/shard_map/all_to_all | solution.py:72
Sparse Core Ops, SparseCore 0:
  23.0 39.8 all-gather.2
  65.0 32.3 all-gather.4

commit v2 on v1

v2 whole, which is shorter than its diff:
```python
import functools

import jax
import jax.numpy as jnp
from jax import lax
from jax.experimental import pallas as pl
from jax.experimental.pallas import tpu as pltpu
from jax.sharding import Mesh, PartitionSpec as P

D = 4096
EPSILON = 1e-06
SWAP = [(0, 1), (1, 0)]
PAIRS = [(i, i ^ 1) for i in range(16)]
LINES = [[0, 2, 4, 6, 9, 11, 13, 15], [1, 3, 5, 7, 8, 10, 12, 14]]
LANES = 128
VMEM_LIMIT = 16 * 1024 * 1024


def mm(a, b):
    return jnp.dot(a, b, preferred_element_type=jnp.float32)


def share_kernel(replica, gate_ref, up_ref, down_ref, near_ref, sems):
    _, depth, units = near_ref.shape
    rest = units - depth
    start = pl.multiple_of(replica[0] * depth, depth)
    rows = pl.ds(start, depth)
    pairs = [
        (gate_ref.at[rows], near_ref.at[0]),
        (up_ref.at[rows], near_ref.at[1]),
        (down_ref.at[pl.ds(0, depth), rows], near_ref.at[2, :, pl.ds(0, depth)]),
    ]
    for i in range(depth // rest):
        columns = pl.ds(pl.multiple_of(start + i * rest, rest), rest)
        pairs.append(
            (down_ref.at[pl.ds(depth, rest), columns], near_ref.at[2, pl.ds(i * rest, rest), pl.ds(depth, rest)])
        )
    copies = [pltpu.make_async_copy(a, b, sems.at[i]) for i, (a, b) in enumerate(pairs)]
    for copy in copies:
        copy.start()
    for copy in copies:
        copy.wait()


def share(replica, replicas, gate, up, down):
    width, units = gate.shape
    here = pl.BlockSpec(memory_space=pltpu.HBM)
    return pl.pallas_call(
        share_kernel,
        in_specs=[pl.BlockSpec(memory_space=pltpu.SMEM), here, here, here],
        out_specs=pl.BlockSpec(memory_space=pltpu.VMEM),
        out_shape=jax.ShapeDtypeStruct((3, width // replicas, units), gate.dtype),
        scratch_shapes=[pltpu.SemaphoreType.DMA((5,))],
        name="share",
    )(replica, gate, up, down)


def project_kernel(x_ref, gain_ref, gate_ref, up_ref, other_ref, send_ref):
    width, units = gate_ref.shape
    pieces = other_ref.shape[0]
    small = width // pieces
    values = x_ref[...].astype(jnp.float32)
    total = jnp.broadcast_to(jnp.sum(values * values, axis=1, keepdims=True), (values.shape[0], LANES))
    scaled = (values * gain_ref[...]).astype(jnp.bfloat16)
    for i, ref in enumerate((gate_ref, up_ref)):
        send_ref[:, i * units : (i + 1) * units] = mm(scaled, ref[...]).astype(jnp.bfloat16)
    for i in range(2):
        sums = mm(scaled[:, :small], other_ref[0, i])
        for piece in range(1, pieces):
            sums += mm(scaled[:, piece * small : (piece + 1) * small], other_ref[piece, i])
        send_ref[:, (2 + i) * units : (3 + i) * units] = sums.astype(jnp.bfloat16)
    high = total.astype(jnp.bfloat16).astype(jnp.float32)
    lane = lax.broadcasted_iota(jnp.int32, total.shape, 1)
    terms = jnp.where(lane == 0, high, jnp.where(lane == 1, total - high, 0.0))
    send_ref[:, 4 * units :] = terms.astype(jnp.bfloat16)


def project(rows, gain, gate, up, other):
    count, width = rows.shape
    units = gate.shape[1]
    near = pl.BlockSpec(memory_space=pltpu.VMEM)
    return pl.pallas_call(
        project_kernel,
        in_specs=[near] * 5,
        out_specs=near,
        out_shape=jax.ShapeDtypeStruct((count, 4 * units + LANES), jnp.bfloat16),
        compiler_params=pltpu.CompilerParams(vmem_limit_bytes=VMEM_LIMIT),
        cost_estimate=pl.CostEstimate(
            flops=8 * count * width * units, bytes_accessed=8 * width * units, transcendentals=0
        ),
        name="project",
    )(rows, gain, gate, up, other)


def expand_kernel(mine_ref, sent_ref, down_ref, other_ref, out_ref):
    units = down_ref.shape[0]

    def both(at, size):
        at = pl.ds(at, size)
        return mine_ref[:, at].astype(jnp.float32) + sent_ref[:, at].astype(jnp.float32)

    total = jnp.sum(both(4 * units, LANES), axis=1, keepdims=True)
    scale = lax.rsqrt(total / D + EPSILON)
    hidden = []
    for piece in range(2):
        gate, up = both(2 * units * piece, units), both(2 * units * piece + units, units)
        hidden.append((jax.nn.silu(gate * scale) * (up * scale)).astype(jnp.bfloat16))
    out = mm(hidden[0], down_ref[...])
    replicas, _, depth, _ = other_ref.shape
    rest = units - depth
    for i in range(replicas):
        part = mm(hidden[1][:, :depth], other_ref[i, 2, :, :depth])
        tail = [mm(hidden[1][:, depth:], other_ref[i, 2, j : j + rest, depth:]) for j in range(0, depth, rest)]
        at = slice(i * depth, (i + 1) * depth)
        out_ref[:, at] = (out[:, at] + part + jnp.concatenate(tail, axis=1)).astype(out_ref.dtype)


def expand(mine, sent, down, other, kind):
    count, (units, width) = mine.shape[0], down.shape
    near = pl.BlockSpec(memory_space=pltpu.VMEM)
    return pl.pallas_call(
        expand_kernel,
        in_specs=[near] * 4,
        out_specs=near,
        out_shape=jax.ShapeDtypeStruct((count, width), kind),
        compiler_params=pltpu.CompilerParams(vmem_limit_bytes=VMEM_LIMIT),
        cost_estimate=pl.CostEstimate(
            flops=4 * count * width * units, bytes_accessed=4 * width * units, transcendentals=count * units
        ),
        name="expand",
    )(mine, sent, down, other)


def shards(states, norm_gain, expert_ids, route_gates, w_gate, w_up, w_down):
    tokens, width = states.shape
    experts = lax.axis_size("z") // 2
    replicas = lax.axis_size("y") * lax.axis_size("core")
    capacity = tokens // 2
    rows = experts * capacity

    replica = lax.axis_index("y") * lax.axis_size("core") + lax.axis_index("core")
    near = share(replica.astype(jnp.int32)[None], replicas, w_gate[0], w_up[0], w_down[0])
    near = lax.ppermute(near, "xh", SWAP)

    flight_ids = jnp.arange(experts, dtype=jnp.int32)
    matches = expert_ids[:, :, None] == flight_ids[None, None, :]
    member = jnp.any(matches, axis=1)
    weight = jnp.sum(jnp.where(matches, route_gates[:, :, None], 0.0), axis=1)
    before = jnp.tril(jnp.ones((tokens, tokens), jnp.float32), -1)
    position = jnp.dot(before, member.astype(jnp.float32)).astype(jnp.int32)
    slots = jnp.where(member, position, capacity)
    slot_ids = jnp.arange(capacity, dtype=jnp.int32)
    placed = slots.T[:, None, :] == slot_ids[None, :, None]
    placed = placed.reshape(rows, tokens)
    packed = mm(placed.astype(jnp.bfloat16), states).astype(jnp.bfloat16)
    near, _ = lax.optimization_barrier((near, packed))
    other = lax.all_gather(near, ("y", "core"), axis=0)
    exchange = functools.partial(
        lax.all_to_all, axis_name="z", split_axis=0, concat_axis=0, axis_index_groups=LINES, tiled=True
    )
    first = exchange(packed.reshape(experts, capacity, width)).reshape(rows, width)
    second = lax.ppermute(first, "z", PAIRS)

    inputs = (norm_gain[None, :], w_gate[0], w_up[0], other)
    send1 = project(first, *inputs)
    send1, second = lax.optimization_barrier((send1, second))
    send2 = project(second, *inputs)
    sent2 = lax.ppermute(send2, "xl", SWAP)
    send1, _ = lax.optimization_barrier((send1, send2))
    sent1 = lax.ppermute(send1, "xl", SWAP)
    out2 = expand(send2, sent2, w_down[0], other, jnp.bfloat16)
    out1 = expand(send1, sent1, w_down[0], other, jnp.float32)
    out = (out1 + lax.ppermute(out2, "z", PAIRS).astype(jnp.float32)).astype(jnp.bfloat16)
    returned = exchange(out.reshape(experts, capacity, width)).reshape(rows, width)

    weighted = jnp.where(placed, jnp.repeat(weight.T, capacity, axis=0), 0.0)
    high = weighted.astype(jnp.bfloat16)
    low = (weighted - high.astype(jnp.float32)).astype(jnp.bfloat16)
    both = lax.dot_general(
        jnp.concatenate([high, low], axis=1),
        returned,
        (((0,), (0,)), ((), ())),
        preferred_element_type=jnp.float32,
    )
    return (both[:tokens] + both[tokens:]).astype(jnp.bfloat16)


def solution(mesh):
    dp, expert, tensor = (mesh.shape[name] for name in ("dp", "expert", "tensor"))
    fine = Mesh(
        mesh.devices.reshape(dp // 2, 2, expert // 2, 2, tensor),
        ("y", "core", "z", "xh", "xl"),
    )
    tokens, slices = ("y", "core", "z", "xh"), ("z", "xh")
    return jax.shard_map(
        shards,
        mesh=fine,
        in_specs=(
            P(tokens, "xl"),
            P("xl"),
            P(tokens, None),
            P(tokens, None),
            P(slices, "xl", None),
            P(slices, "xl", None),
            P(slices, None, "xl"),
        ),
        out_specs=P(tokens, "xl"),
        check_vma=False,
    )
```

time: 200 us -> 164 us (0.82)
  the two profiles are of different devices: /device:TPU:4 before, /device:TPU:2 now
where the time goes in v2:
time: 164 us; the launch traced here: 163 us
  waiting for transfers between devices  65.9 us (40%)
  blocking collectives  44.4 us (27%)
  starting transfers between devices  25 us (15%)
  between operations  13.6 us (8%)
  Pallas kernels  8.56 us (5%)
  local copies, waits for them, and re-layouts  2.6 us (2%)
  other arithmetic  1.65 us (1%)
    all_to_all x1, blocking collectives, shards(): exchange(packed.reshape(experts, capacity, width)).reshape(rows, width)  44.4 us
    all_to_all x1, waiting for transfers between devices, shards(): exchange(out.reshape(experts, capacity, width)).reshape(rows, width)  30.1 us
    ppermute x1, waiting for transfers between devices, shards(): near = lax.ppermute(near, 'xh', SWAP)  13 us
    all_to_all x1, starting transfers between devices, shards(): exchange(out.reshape(experts, capacity, width)).reshape(rows, width)  10.6 us
    ppermute x1, waiting for transfers between devices, shards(): sent2 = lax.ppermute(send2, 'xl', SWAP)  8.61 us
    ppermute x1, waiting for transfers between devices, shards(): sent1 = lax.ppermute(send1, 'xl', SWAP)  7.57 us
    ppermute x1, waiting for transfers between devices, shards(): second = lax.ppermute(first, 'z', PAIRS)  6.56 us
    pallas_call x2, Pallas kernels, project(): pl.pallas_call(project_kernel, in_specs=[near] * 5, out_specs=near, out_s...  4.74 us
  transfers between devices with their start and end apart: 7, of which 5 were waited for; matrix products, arithmetic and copies ran while one was open for 1% of the time, Pallas kernels for 2%

profile of v2, /device:TPU:2, one launch (start us, length us, event | category | flops | bytes accessed | tf_op | source)
XLA Modules:
  0.0 163.3 jit_solution(8373974571821780658)
XLA Ops:
  6.6 2.1 %share.1 = bf16[3,256,384]{2,1,0:T(8,128)(2,1)} custom-call(s32[1]{0:T(128)} %bitcast.9.replica, bf16[2048,384]{1,0:T(8,128)(2,1)} %bitcast.23, bf16[2048,384]{1,0:T(8,128)(2,1)} %bitcast.26, bf16[384,2048]{1,0:T(8,128)(2,1)} %bitcast.29), custom_call_target="tpu_custom_call" | custom-call | tf_op jit(solution)/shard_map/share/pallas_call | solution.py:48
  8.7 0.0 copy-start.3
  8.7 0.0 copy-start.6
  8.7 4.2 %collective-permute-start = (bf16[3,256,384]{2,1,0:T(8,128)(2,1)}, bf16[3,256,384]{2,1,0:T(8,128)(2,1)}, u32[]{:S(2)}, u32[]{:S(2)}) collective-permute-start(bf16[3,256,384]{2,1,0:T(8,128)(2,1)} %share.1), channel_id=1, source_target_pairs={{0,2},{2,0},{1,3},{3,1},{4,6},{6,4},{5,7},{7,5},{8,10},{10,8},{9,1... | collective-permute-start | bytes 1769480 | tf_op jit(solution)/shard_map/ppermute | solution.py:143
  12.9 0.1 eq.39
  13.0 0.1 copy.15
  13.1 0.2 fusion
  13.3 0.1 copy.14
  13.4 1.2 convolution_convert_fusion
  14.6 13.0 %collective-permute-done = bf16[3,256,384]{2,1,0:T(8,128)(2,1)} collective-permute-done((bf16[3,256,384]{2,1,0:T(8,128)(2,1)}, bf16[3,256,384]{2,1,0:T(8,128)(2,1)}, u32[]{:S(2)}, u32[]{:S(2)}) %collective-permute-start) | collective-permute-done | bytes 589856 | tf_op jit(solution)/shard_map/ppermute | solution.py:143
  27.6 0.0 all-gather.3.cloned.1.call-update
  27.6 44.4 %all_to_all.10 = bf16[8,16,2048]{2,1,0:T(8,128)(2,1)} all-to-all(bf16[8,16,2048]{2,1,0:T(8,128)(2,1)} %bitcast.34), channel_id=1, replica_groups={{0,8,16,24,36,44,52,60},{4,12,20,28,32,40,48,56},{1,9,17,25,37,45,53,61..., dimensions={0} | all-to-all | bytes 1048576 | tf_op jit(solution)/shard_map/all_to_all | solution.py:161
  72.0 3.0 %collective-permute-start.1 = (bf16[128,2048]{1,0:T(8,128)(2,1)}, bf16[128,2048]{1,0:T(8,128)(2,1)}, u32[]{:S(2)}, u32[]{:S(2)}) collective-permute-start(bf16[128,2048]{1,0:T(8,128)(2,1)} %bitcast.5.x_ref), channel_id=1, source_target_pairs={{0,4},{4,0},{8,12},{12,8},{16,20},{20,16},{24,28},{28,24},{32,36},... | collective-permute-start | bytes 1572872 | tf_op jit(solution)/shard_map/ppermute | solution.py:162
  75.0 0.0 all-gather.3.cloned.1.call-done
  75.1 2.3 %copy-done.1 = bf16[24,256,384]{2,1,0:T(8,128)(2,1)S(1)} copy-done((bf16[24,256,384]{2,1,0:T(8,128)(2,1)S(1)}, bf16[24,256,384]{2,1,0:T(8,128)(2,1)}, u32[]{:S(2)}) %copy-start.1) | copy-done | bytes 4718616
  77.4 2.4 %project.2.mine_ref = bf16[128,1664]{1,0:T(8,128)(2,1)S(1)} custom-call(bf16[128,2048]{1,0:T(8,128)(2,1)} %bitcast.5.x_ref, f32[1,2048]{1,0:T(1,128)S(1)} %bitcast.32, bf16[2048,384]{1,0:T(8,128)(2,1)S(1)} %bitcast.24, bf16[2048,384]{1,0:T(8,128)(2,1)S(1)} %bitcast.27, bf16[8,3,256,384]{3,2,1,0:T(8,128)(2,1)S(1)} %bitcast.19), custom_call_target="tpu_custom_call" | custom-call | flops 805306368 | bytes 6291456 | tf_op jit(solution)/shard_map/project/pallas_call | solution.py:82
  79.9 0.0 copy-start.5
  79.9 6.6 %collective-permute-done.1.x_ref = bf16[128,2048]{1,0:T(8,128)(2,1)} collective-permute-done((bf16[128,2048]{1,0:T(8,128)(2,1)}, bf16[128,2048]{1,0:T(8,128)(2,1)}, u32[]{:S(2)}, u32[]{:S(2)}) %collective-permute-start.1) | collective-permute-done | bytes 524320 | tf_op jit(solution)/shard_map/ppermute | solution.py:162
  86.4 2.3 %project.3.mine_ref = bf16[128,1664]{1,0:T(8,128)(2,1)S(1)} custom-call(bf16[128,2048]{1,0:T(8,128)(2,1)} %collective-permute-done.1.x_ref, f32[1,2048]{1,0:T(1,128)S(1)} %bitcast.33, bf16[2048,384]{1,0:T(8,128)(2,1)S(1)} %bitcast.25, bf16[2048,384]{1,0:T(8,128)(2,1)S(1)} %bitcast.28, bf16[8,3,256,384]{3,2,1,0:T(8,128)(2,1)S(1)} %bitcast.20), custom_call_target="tpu_custom_call" | custom-call | flops 805306368 | bytes 6291456 | tf_op jit(solution)/shard_map/project/pallas_call | solution.py:82
  88.7 2.4 %collective-permute-start.3 = (bf16[128,1664]{1,0:T(8,128)(2,1)S(1)}, bf16[128,1664]{1,0:T(8,128)(2,1)S(1)}, u32[]{:S(2)}, u32[]{:S(2)}) collective-permute-start(bf16[128,1664]{1,0:T(8,128)(2,1)S(1)} %project.3.mine_ref), channel_id=1, source_target_pairs={{0,1},{1,0},{2,3},{3,2},{4,5},{5,4},{6,7},{7,6},{8,9},{9,8},{10,11... | collective-permute-start | bytes 1277960 | tf_op jit(solution)/shard_map/ppermute | solution.py:168
  91.2 8.6 %collective-permute-done.3.sent_ref = bf16[128,1664]{1,0:T(8,128)(2,1)S(1)} collective-permute-done((bf16[128,1664]{1,0:T(8,128)(2,1)S(1)}, bf16[128,1664]{1,0:T(8,128)(2,1)S(1)}, u32[]{:S(2)}, u32[]{:S(2)}) %collective-permute-start.3) | collective-permute-done | bytes 426016 | tf_op jit(solution)/shard_map/ppermute | solution.py:168
  99.8 0.9 expand.3
  100.7 2.4 %collective-permute-start.4 = (bf16[128,2048]{1,0:T(8,128)(2,1)S(1)}, bf16[128,2048]{1,0:T(8,128)(2,1)S(1)}, u32[]{:S(2)}, u32[]{:S(2)}) collective-permute-start(bf16[128,2048]{1,0:T(8,128)(2,1)S(1)} %expand.3), channel_id=1, source_target_pairs={{0,4},{4,0},{8,12},{12,8},{16,20},{20,16},{24,28},{28,24},{32,36},... | collective-permute-start | bytes 1572872 | tf_op jit(solution)/shard_map/ppermute | solution.py:173
  103.1 2.4 %collective-permute-start.2 = (bf16[128,1664]{1,0:T(8,128)(2,1)S(1)}, bf16[128,1664]{1,0:T(8,128)(2,1)S(1)}, u32[]{:S(2)}, u32[]{:S(2)}) collective-permute-start(bf16[128,1664]{1,0:T(8,128)(2,1)S(1)} %project.2.mine_ref), channel_id=1, source_target_pairs={{0,1},{1,0},{2,3},{3,2},{4,5},{5,4},{6,7},{7,6},{8,9},{9,8},{10,11... | collective-permute-start | bytes 1277960 | tf_op jit(solution)/shard_map/ppermute | solution.py:170
  105.5 7.6 %collective-permute-done.2.sent_ref = bf16[128,1664]{1,0:T(8,128)(2,1)S(1)} collective-permute-done((bf16[128,1664]{1,0:T(8,128)(2,1)S(1)}, bf16[128,1664]{1,0:T(8,128)(2,1)S(1)}, u32[]{:S(2)}, u32[]{:S(2)}) %collective-permute-start.2) | collective-permute-done | bytes 426016 | tf_op jit(solution)/shard_map/ppermute | solution.py:170
  113.1 0.9 expand.2
  114.0 0.0 collective-permute-done.4
  114.0 0.9 add_convert_fusion
  114.9 10.6 %all-to-all-start.1 = ((bf16[8,16,2048]{2,1,0:T(8,128)(2,1)}), bf16[8,16,2048]{2,1,0:T(8,128)(2,1)S(1)}, u32[]{:S(2)}, u32[]{:S(2)}) async-start(bf16[8,16,2048]{2,1,0:T(8,128)(2,1)} %bitcast.12), calls=%async_computation.1 | async-start | bytes 1048576 | tf_op jit(solution)/shard_map/all_to_all | solution.py:174
  125.5 30.1 %all-to-all-done.1 = bf16[8,16,2048]{2,1,0:T(8,128)(2,1)S(1)} async-done(((bf16[8,16,2048]{2,1,0:T(8,128)(2,1)}), bf16[8,16,2048]{2,1,0:T(8,128)(2,1)S(1)}, u32[]{:S(2)}, u32[]{:S(2)}) %all-to-all-start.1) | async-done | bytes 524320 | tf_op jit(solution)/shard_map/all_to_all | solution.py:174
  155.6 0.2 fusion.3
  155.8 0.7 fusion.1
  (23 shorter events, 0.1 us)
Async XLA Ops:
  6.5 6.9 %copy-start = (bf16[32,2048]{1,0:T(8,128)(2,1)S(1)}, bf16[32,2048]{1,0:T(8,128)(2,1)}, u32[]{:S(2)}) copy-start(bf16[32,2048]{1,0:T(8,128)(2,1)} %param.7) | copy-start | bytes 393220
  6.5 68.5 %all-gather.3.cloned.1.call-start = ((), (), s32[]{:S(2)}) async-start(), calls=%async_computation.2 | async-start | bytes 5308416 | tf_op jit(solution)/shard_map/all_gather | solution.py:157
  6.5 6.3 %copy-start.7 = (s32[32,8]{0,1:T(8,128)S(1)}, s32[32,8]{0,1:T(8,128)}, u32[]{:S(2)}) copy-start(s32[32,8]{0,1:T(8,128)} %param.9) | copy-start | bytes 3076
  6.5 6.3 %copy-start.8 = (f32[32,8]{0,1:T(8,128)S(1)}, f32[32,8]{0,1:T(8,128)}, u32[]{:S(2)}) copy-start(f32[32,8]{0,1:T(8,128)} %param.10) | copy-start | bytes 3076
  6.5 68.5 %copy-start.4 = (bf16[1,2048,384]{2,1,0:T(8,128)(2,1)S(1)}, bf16[1,2048,384]{2,1,0:T(8,128)(2,1)}, u32[]{:S(2)}) copy-start(bf16[1,2048,384]{2,1,0:T(8,128)(2,1)} %param.12) | copy-start | bytes 4718596
  8.7 66.4 %copy-start.3 = (bf16[1,2048,384]{2,1,0:T(8,128)(2,1)S(1)}, bf16[1,2048,384]{2,1,0:T(8,128)(2,1)}, u32[]{:S(2)}) copy-start(bf16[1,2048,384]{2,1,0:T(8,128)(2,1)} %param.11) | copy-start | bytes 4718596
  8.7 66.4 %copy-start.6 = (f32[2048]{0:T(1024)S(1)}, f32[2048]{0:T(1024)}, u32[]{:S(2)}) copy-start(f32[2048]{0:T(1024)} %param.8) | copy-start | bytes 24580
  8.7 18.9 %collective-permute-start = (bf16[3,256,384]{2,1,0:T(8,128)(2,1)}, bf16[3,256,384]{2,1,0:T(8,128)(2,1)}, u32[]{:S(2)}, u32[]{:S(2)}) collective-permute-start(bf16[3,256,384]{2,1,0:T(8,128)(2,1)} %share.1), channel_id=1, source_target_pairs={{0,2},{2,0},{1,3},{3,1},{4,6},{6,4},{5,7},{7,5},{8,10},{10,8},{9,1... | collective-permute-start | bytes 1769480 | tf_op jit(solution)/shard_map/ppermute | solution.py:143
  72.0 14.4 %collective-permute-start.1 = (bf16[128,2048]{1,0:T(8,128)(2,1)}, bf16[128,2048]{1,0:T(8,128)(2,1)}, u32[]{:S(2)}, u32[]{:S(2)}) collective-permute-start(bf16[128,2048]{1,0:T(8,128)(2,1)} %bitcast.5.x_ref), channel_id=1, source_target_pairs={{0,4},{4,0},{8,12},{12,8},{16,20},{20,16},{24,28},{28,24},{32,36},... | collective-permute-start | bytes 1572872 | tf_op jit(solution)/shard_map/ppermute | solution.py:162
  75.1 2.3 %copy-start.1 = (bf16[24,256,384]{2,1,0:T(8,128)(2,1)S(1)}, bf16[24,256,384]{2,1,0:T(8,128)(2,1)}, u32[]{:S(2)}) copy-start(bf16[24,256,384]{2,1,0:T(8,128)(2,1)} %all-gather.3.cloned.1.call-done) | copy-start | bytes 14155780
  77.4 9.0 %copy-start.2 = (bf16[24,256,384]{2,1,0:T(8,128)(2,1)S(1)}, bf16[24,256,384]{2,1,0:T(8,128)(2,1)}, u32[]{:S(2)}) copy-start(bf16[24,256,384]{2,1,0:T(8,128)(2,1)} %all-gather.3.cloned.1.call-done) | copy-start | bytes 14155780
  79.9 19.9 %copy-start.5 = (bf16[1,384,2048]{2,1,0:T(8,128)(2,1)S(1)}, bf16[1,384,2048]{2,1,0:T(8,128)(2,1)}, u32[]{:S(2)}) copy-start(bf16[1,384,2048]{2,1,0:T(8,128)(2,1)} %param.13) | copy-start | bytes 4718596
  88.7 11.1 %collective-permute-start.3 = (bf16[128,1664]{1,0:T(8,128)(2,1)S(1)}, bf16[128,1664]{1,0:T(8,128)(2,1)S(1)}, u32[]{:S(2)}, u32[]{:S(2)}) collective-permute-start(bf16[128,1664]{1,0:T(8,128)(2,1)S(1)} %project.3.mine_ref), channel_id=1, source_target_pairs={{0,1},{1,0},{2,3},{3,2},{4,5},{5,4},{6,7},{7,6},{8,9},{9,8},{10,11... | collective-permute-start | bytes 1277960 | tf_op jit(solution)/shard_map/ppermute | solution.py:168
  100.7 13.3 %collective-permute-start.4 = (bf16[128,2048]{1,0:T(8,128)(2,1)S(1)}, bf16[128,2048]{1,0:T(8,128)(2,1)S(1)}, u32[]{:S(2)}, u32[]{:S(2)}) collective-permute-start(bf16[128,2048]{1,0:T(8,128)(2,1)S(1)} %expand.3), channel_id=1, source_target_pairs={{0,4},{4,0},{8,12},{12,8},{16,20},{20,16},{24,28},{28,24},{32,36},... | collective-permute-start | bytes 1572872 | tf_op jit(solution)/shard_map/ppermute | solution.py:173
  103.1 10.0 %collective-permute-start.2 = (bf16[128,1664]{1,0:T(8,128)(2,1)S(1)}, bf16[128,1664]{1,0:T(8,128)(2,1)S(1)}, u32[]{:S(2)}, u32[]{:S(2)}) collective-permute-start(bf16[128,1664]{1,0:T(8,128)(2,1)S(1)} %project.2.mine_ref), channel_id=1, source_target_pairs={{0,1},{1,0},{2,3},{3,2},{4,5},{5,4},{6,7},{7,6},{8,9},{9,8},{10,11... | collective-permute-start | bytes 1277960 | tf_op jit(solution)/shard_map/ppermute | solution.py:170
  114.9 40.7 %all-to-all-start.1 = ((bf16[8,16,2048]{2,1,0:T(8,128)(2,1)}), bf16[8,16,2048]{2,1,0:T(8,128)(2,1)S(1)}, u32[]{:S(2)}, u32[]{:S(2)}) async-start(bf16[8,16,2048]{2,1,0:T(8,128)(2,1)} %bitcast.12), calls=%async_computation.1 | async-start | bytes 1048576 | tf_op jit(solution)/shard_map/all_to_all | solution.py:174
Sparse Core Ops, SparseCore 0:
  27.7 46.4 all-gather.2

commit v3 on v2

--- a/solution.py
+++ b/solution.py
@@ -13,7 +13,10 @@
 PAIRS = [(i, i ^ 1) for i in range(16)]
 LINES = [[0, 2, 4, 6, 9, 11, 13, 15], [1, 3, 5, 7, 8, 10, 12, 14]]
 LANES = 128
-VMEM_LIMIT = 16 * 1024 * 1024
+VMEM_LIMIT = 52 * 1024 * 1024
+EXPAND_FLOPS = 402653184
+WAIT_FLOPS = 1107000000
+SCALE_FLOPS = 70848000000
 
 
 def mm(a, b):
@@ -51,81 +54,150 @@
         out_specs=pl.BlockSpec(memory_space=pltpu.VMEM),
         out_shape=jax.ShapeDtypeStruct((3, width // replicas, units), gate.dtype),
         scratch_shapes=[pltpu.SemaphoreType.DMA((5,))],
+        compiler_params=pltpu.CompilerParams(vmem_limit_bytes=VMEM_LIMIT),
         name="share",
     )(replica, gate, up, down)
 
 
-def project_kernel(x_ref, gain_ref, gate_ref, up_ref, other_ref, send_ref):
-    width, units = gate_ref.shape
-    pieces = other_ref.shape[0]
-    small = width // pieces
-    values = x_ref[...].astype(jnp.float32)
+def squares(values):
     total = jnp.broadcast_to(jnp.sum(values * values, axis=1, keepdims=True), (values.shape[0], LANES))
-    scaled = (values * gain_ref[...]).astype(jnp.bfloat16)
-    for i, ref in enumerate((gate_ref, up_ref)):
-        send_ref[:, i * units : (i + 1) * units] = mm(scaled, ref[...]).astype(jnp.bfloat16)
-    for i in range(2):
-        sums = mm(scaled[:, :small], other_ref[0, i])
-        for piece in range(1, pieces):
-            sums += mm(scaled[:, piece * small : (piece + 1) * small], other_ref[piece, i])
-        send_ref[:, (2 + i) * units : (3 + i) * units] = sums.astype(jnp.bfloat16)
     high = total.astype(jnp.bfloat16).astype(jnp.float32)
     lane = lax.broadcasted_iota(jnp.int32, total.shape, 1)
-    terms = jnp.where(lane == 0, high, jnp.where(lane == 1, total - high, 0.0))
-    send_ref[:, 4 * units :] = terms.astype(jnp.bfloat16)
-
-
-def project(rows, gain, gate, up, other):
-    count, width = rows.shape
-    units = gate.shape[1]
-    near = pl.BlockSpec(memory_space=pltpu.VMEM)
-    return pl.pallas_call(
-        project_kernel,
-        in_specs=[near] * 5,
+    return jnp.where(lane == 0, high, jnp.where(lane == 1, total - high, 0.0)).astype(jnp.bfloat16)
+
+
+def near_kernel(x_ref, gain_ref, gate_ref, up_ref, scaled_ref, send_ref, weights, sems):
+    width, units = gate_ref.shape
+    half = width // 2
+    copies = []
+    for step in range(2):
+        rows = pl.ds(step * half, half)
+        for i, ref in enumerate((gate_ref, up_ref)):
+            copies.append(pltpu.make_async_copy(ref.at[rows], weights.at[i, rows], sems.at[step, i]))
+            copies[-1].start()
+    values = x_ref[...].astype(jnp.float32)
+    send_ref[:, 2 * units :] = squares(values)
+    scaled_ref[...] = (values * gain_ref[...]).astype(jnp.bfloat16)
+    copies[0].wait()
+    copies[1].wait()
+    totals = [mm(scaled_ref[:, :half], weights[i, :half]) for i in range(2)]
+    copies[2].wait()
+    copies[3].wait()
+    for i in range(2):
+        total = totals[i] + mm(scaled_ref[:, half:], weights[i, half:])
+        send_ref[:, i * units : (i + 1) * units] = total.astype(jnp.bfloat16)
+
+
+def project_near(rows, gain, gate, up, flops):
+    (count, width), units = rows.shape, gate.shape[1]
+    near, here = pl.BlockSpec(memory_space=pltpu.VMEM), pl.BlockSpec(memory_space=pltpu.HBM)
+    return pl.pallas_call(
+        near_kernel,
+        in_specs=[near] * 2 + [here] * 2,
+        out_specs=[near] * 2,
+        out_shape=[
+            jax.ShapeDtypeStruct((count, width), jnp.bfloat16),
+            jax.ShapeDtypeStruct((count, 2 * units + LANES), jnp.bfloat16),
+        ],
+        scratch_shapes=[pltpu.VMEM((2, width, units), jnp.bfloat16), pltpu.SemaphoreType.DMA((2, 2))],
+        compiler_params=pltpu.CompilerParams(vmem_limit_bytes=VMEM_LIMIT),
+        cost_estimate=pl.CostEstimate(flops=flops, bytes_accessed=4 * width * units, transcendentals=0),
+        name="project_near",
+    )(rows, gain, gate, up)
+
+
+def far_kernel(scaled_ref, near_ref, other_ref, send_ref, weights, sems):
+    pieces, _, depth, units = other_ref.shape
+    half, copies = pieces // 2, []
+    for piece in range(pieces):
+        for i in range(2):
+            rows = pl.ds(piece * depth, depth)
+            copies.append(pltpu.make_async_copy(other_ref.at[piece, i], weights.at[i, rows], sems.at[piece, i]))
+            copies[-1].start()
+    kept = near_ref.shape[1]
+    send_ref[:, :kept] = near_ref[...]
+    totals = [None] * 2
+    for step in range(2):
+        for copy in copies[step * pieces : (step + 1) * pieces]:
+            copy.wait()
+        rows = slice(step * half * depth, (step + 1) * half * depth)
+        for i in range(2):
+            product = mm(scaled_ref[:, rows], weights[i, rows])
+            totals[i] = product if step == 0 else totals[i] + product
+    for i in range(2):
+        send_ref[:, kept + i * units : kept + (i + 1) * units] = totals[i].astype(jnp.bfloat16)
+
+
+def project_far(scaled, near_send, other):
+    (count, width), (pieces, _, _, units) = scaled.shape, other.shape
+    near, here = pl.BlockSpec(memory_space=pltpu.VMEM), pl.BlockSpec(memory_space=pltpu.HBM)
+    return pl.pallas_call(
+        far_kernel,
+        in_specs=[near] * 2 + [here],
         out_specs=near,
-        out_shape=jax.ShapeDtypeStruct((count, 4 * units + LANES), jnp.bfloat16),
+        out_shape=jax.ShapeDtypeStruct((count, near_send.shape[1] + 2 * units), jnp.bfloat16),
+        scratch_shapes=[pltpu.VMEM((2, width, units), jnp.bfloat16), pltpu.SemaphoreType.DMA((pieces, 2))],
         compiler_params=pltpu.CompilerParams(vmem_limit_bytes=VMEM_LIMIT),
         cost_estimate=pl.CostEstimate(
-            flops=8 * count * width * units, bytes_accessed=8 * width * units, transcendentals=0
+            flops=4 * count * width * units, bytes_accessed=4 * width * units, transcendentals=0
         ),
-        name="project",
-    )(rows, gain, gate, up, other)
-
-
-def expand_kernel(mine_ref, sent_ref, down_ref, other_ref, out_ref):
-    units = down_ref.shape[0]
+        name="project_far",
+    )(scaled, near_send, other)
+
+
+def expand_kernel(mine_ref, sent_ref, down_ref, other_ref, out_ref, down, hidden_ref, sems):
+    units, width = down_ref.shape
+    replicas, _, depth, _ = other_ref.shape
+    rest = units - depth
+    pairs = [(down_ref, down.at[pl.ds(0, units)])]
+    for i in range(replicas):
+        pairs.append(
+            (other_ref.at[i, 2, :, pl.ds(0, depth)], down.at[pl.ds(units, depth), pl.ds(i * depth, depth)])
+        )
+        for j in range(0, depth, rest):
+            pairs.append(
+                (
+                    other_ref.at[i, 2, pl.ds(j, rest), pl.ds(depth, rest)],
+                    down.at[pl.ds(units + depth, rest), pl.ds(i * depth + j, rest)],
+                )
+            )
+    copies = [pltpu.make_async_copy(a, b, sems.at[i]) for i, (a, b) in enumerate(pairs)]
+    for copy in copies:
+        copy.start()
 
     def both(at, size):
         at = pl.ds(at, size)
         return mine_ref[:, at].astype(jnp.float32) + sent_ref[:, at].astype(jnp.float32)
 
-    total = jnp.sum(both(4 * units, LANES), axis=1, keepdims=True)
+    total = jnp.sum(both(2 * units, LANES), axis=1, keepdims=True)
     scale = lax.rsqrt(total / D + EPSILON)
-    hidden = []
     for piece in range(2):
-        gate, up = both(2 * units * piece, units), both(2 * units * piece + units, units)
-        hidden.append((jax.nn.silu(gate * scale) * (up * scale)).astype(jnp.bfloat16))
-    out = mm(hidden[0], down_ref[...])
-    replicas, _, depth, _ = other_ref.shape
-    rest = units - depth
-    for i in range(replicas):
-        part = mm(hidden[1][:, :depth], other_ref[i, 2, :, :depth])
-        tail = [mm(hidden[1][:, depth:], other_ref[i, 2, j : j + rest, depth:]) for j in range(0, depth, rest)]
-        at = slice(i * depth, (i + 1) * depth)
-        out_ref[:, at] = (out[:, at] + part + jnp.concatenate(tail, axis=1)).astype(out_ref.dtype)
-
-
-def expand(mine, sent, down, other, kind):
+        at = piece * (2 * units + LANES)
+        gate, up = both(at, units), both(at + units, units)
+        hidden = jax.nn.silu(gate * scale) * (up * scale)
+        hidden_ref[:, units * piece : units * (piece + 1)] = hidden.astype(jnp.bfloat16)
+    for copy in copies:
+        copy.wait()
+    out_ref[...] = mm(hidden_ref[...], down[...]).astype(out_ref.dtype)
+
+
+def expand(mine, sent, down, other, kind, flops):
     count, (units, width) = mine.shape[0], down.shape
-    near = pl.BlockSpec(memory_space=pltpu.VMEM)
+    near, here = pl.BlockSpec(memory_space=pltpu.VMEM), pl.BlockSpec(memory_space=pltpu.HBM)
+    replicas, _, depth, _ = other.shape
     return pl.pallas_call(
         expand_kernel,
-        in_specs=[near] * 4,
+        in_specs=[near] * 2 + [here] * 2,
         out_specs=near,
         out_shape=jax.ShapeDtypeStruct((count, width), kind),
+        scratch_shapes=[
+            pltpu.VMEM((2 * units, width), jnp.bfloat16),
+            pltpu.VMEM((count, 2 * units), jnp.bfloat16),
+            pltpu.SemaphoreType.DMA((1 + replicas * (1 + depth // (units - depth)),)),
+        ],
         compiler_params=pltpu.CompilerParams(vmem_limit_bytes=VMEM_LIMIT),
         cost_estimate=pl.CostEstimate(
-            flops=4 * count * width * units, bytes_accessed=4 * width * units, transcendentals=count * units
+            flops=flops, bytes_accessed=4 * width * units, transcendentals=count * units
         ),
         name="expand",
     )(mine, sent, down, other)
@@ -161,15 +233,18 @@
     first = exchange(packed.reshape(experts, capacity, width)).reshape(rows, width)
     second = lax.ppermute(first, "z", PAIRS)
 
-    inputs = (norm_gain[None, :], w_gate[0], w_up[0], other)
-    send1 = project(first, *inputs)
-    send1, second = lax.optimization_barrier((send1, second))
-    send2 = project(second, *inputs)
+    gain = norm_gain[None, :]
+    gate, up = w_gate[0], w_up[0]
+    scaled1, near1 = project_near(first, gain, gate, up, SCALE_FLOPS)
+    near1, second = lax.optimization_barrier((near1, second))
+    scaled2, near2 = project_near(second, gain, gate, up, EXPAND_FLOPS)
+    send2 = project_far(scaled2, near2, other)
     sent2 = lax.ppermute(send2, "xl", SWAP)
-    send1, _ = lax.optimization_barrier((send1, send2))
+    near1, _ = lax.optimization_barrier((near1, send2))
+    send1 = project_far(scaled1, near1, other)
     sent1 = lax.ppermute(send1, "xl", SWAP)
-    out2 = expand(send2, sent2, w_down[0], other, jnp.bfloat16)
-    out1 = expand(send1, sent1, w_down[0], other, jnp.float32)
+    out2 = expand(send2, sent2, w_down[0], other, jnp.bfloat16, EXPAND_FLOPS)
+    out1 = expand(send1, sent1, w_down[0], other, jnp.float32, WAIT_FLOPS)
     out = (out1 + lax.ppermute(out2, "z", PAIRS).astype(jnp.float32)).astype(jnp.bfloat16)
     returned = exchange(out.reshape(experts, capacity, width)).reshape(rows, width)
 

time: 164 us -> 158 us (0.963)
  blocking collectives: 44.4 us -> 0 us
  starting transfers between devices: 25 us -> 41.8 us
  waiting for transfers between devices: 65.9 us -> 80.6 us
  Pallas kernels: 8.56 us -> 17.3 us
    all_to_all x1 -> x0, blocking collectives: 44.4 us -> none  [shards(): exchange(packed.reshape(experts, capacity, width)).reshape(rows, width)]
    all_to_all x0 -> x1, waiting for transfers between devices: none -> 29.7 us  [shards(): exchange(packed.reshape(experts, capacity, width)).reshape(rows, width)]
    all_to_all x0 -> x1, starting transfers between devices: none -> 14.6 us  [shards(): exchange(packed.reshape(experts, capacity, width)).reshape(rows, width)]
    ppermute x1, waiting for transfers between devices: 13 us -> 0.01 us  [shards(): near = lax.ppermute(near, 'xh', SWAP)]
    pallas_call x4 -> x6, Pallas kernels: 6.48 us -> 16.1 us  [the longest x2 5.57 us: project_far(): pl.pallas_call(far_kernel, in_specs=[near] * 2 + [here], out_specs=near,...]
    ppermute x1, waiting for transfers between devices: 7.57 us -> 1.91 us  [shards(): sent1 = lax.ppermute(send1, 'xl', SWAP)]
    ppermute x1, waiting for transfers between devices: 0.01 us -> 5.4 us  [shards(): lax.ppermute(out2, 'z', PAIRS).astype(jnp.float32)]
    ppermute x1, waiting for transfers between devices: 8.61 us -> 6 us  [shards(): sent2 = lax.ppermute(send2, 'xl', SWAP)]
  transfers between devices with their start and end apart: 7 -> 8, of which waited for: 5 -> 6; matrix products, arithmetic and copies ran while one was open for 1% -> 1% of each run, Pallas kernels for 2% -> 8%
where the time goes in v3:
time: 158 us
  waiting for transfers between devices  80.6 us (51%)
  starting transfers between devices  41.8 us (26%)
  Pallas kernels  17.3 us (11%)
  between operations  13.6 us (9%)
  other arithmetic  1.65 us (1%)
  matrix products  1.58 us (1%)
    all_to_all x1, waiting for transfers between devices, shards(): exchange(packed.reshape(experts, capacity, width)).reshape(rows, width)  29.7 us
    all_to_all x1, waiting for transfers between devices, shards(): exchange(out.reshape(experts, capacity, width)).reshape(rows, width)  29.5 us
    all_to_all x1, starting transfers between devices, shards(): exchange(packed.reshape(experts, capacity, width)).reshape(rows, width)  14.6 us
    all_to_all x1, starting transfers between devices, shards(): exchange(out.reshape(experts, capacity, width)).reshape(rows, width)  12 us
    ppermute x1, waiting for transfers between devices, shards(): second = lax.ppermute(first, 'z', PAIRS)  8.06 us
    ppermute x1, waiting for transfers between devices, shards(): sent2 = lax.ppermute(send2, 'xl', SWAP)  6 us
    pallas_call x2, Pallas kernels, project_far(): pl.pallas_call(far_kernel, in_specs=[near] * 2 + [here], out_specs=near,...  5.57 us
    ppermute x1, waiting for transfers between devices, shards(): lax.ppermute(out2, 'z', PAIRS).astype(jnp.float32)  5.4 us
  transfers between devices with their start and end apart: 8, of which 6 were waited for; matrix products, arithmetic and copies ran while one was open for 1% of the time, Pallas kernels for 8%

profile of v3, /device:TPU:2, one launch (start us, length us, event | category | flops | bytes accessed | tf_op | source)
XLA Modules:
  0.0 157.7 jit_solution(16226477845977626576)
XLA Ops:
  6.5 1.2 share.1
  7.7 4.0 %collective-permute-start.1 = (bf16[3,256,384]{2,1,0:T(8,128)(2,1)S(1)}, bf16[3,256,384]{2,1,0:T(8,128)(2,1)S(1)}, u32[]{:S(2)}, u32[]{:S(2)}) collective-permute-start(bf16[3,256,384]{2,1,0:T(8,128)(2,1)S(1)} %share.1), channel_id=1, source_target_pairs={{0,2},{2,0},{1,3},{3,1},{4,6},{6,4},{5,7},{7,5},{8,10},{10,8},{9,1... | collective-permute-start | bytes 1769480 | tf_op jit(solution)/shard_map/ppermute | solution.py:215
  11.9 0.1 eq.39
  11.9 0.1 copy.15
  12.0 0.2 fusion
  12.2 0.1 copy.14
  12.3 1.2 convolution_convert_fusion
  13.5 14.6 %all-to-all-start = ((bf16[8,16,2048]{2,1,0:T(8,128)(2,1)}), bf16[8,16,2048]{2,1,0:T(8,128)(2,1)S(1)}, u32[]{:S(2)}, u32[]{:S(2)}) async-start(bf16[8,16,2048]{2,1,0:T(8,128)(2,1)} %bitcast.4), calls=%async_computation | async-start | bytes 1048576 | tf_op jit(solution)/shard_map/all_to_all | solution.py:233
  28.1 0.0 all-gather.3.cloned.1.call-start
  28.2 0.8 copy-done.2
  29.0 0.0 all-gather.3.cloned.1.call-update
  29.1 29.7 %all-to-all-done = bf16[8,16,2048]{2,1,0:T(8,128)(2,1)S(1)} async-done(((bf16[8,16,2048]{2,1,0:T(8,128)(2,1)}), bf16[8,16,2048]{2,1,0:T(8,128)(2,1)S(1)}, u32[]{:S(2)}, u32[]{:S(2)}) %all-to-all-start) | async-done | bytes 524320 | tf_op jit(solution)/shard_map/all_to_all | solution.py:233
  58.7 2.4 %collective-permute-start = (bf16[128,2048]{1,0:T(8,128)(2,1)S(1)}, bf16[128,2048]{1,0:T(8,128)(2,1)S(1)}, u32[]{:S(2)}, u32[]{:S(2)}) collective-permute-start(bf16[128,2048]{1,0:T(8,128)(2,1)S(1)} %bitcast.19), channel_id=1, source_target_pairs={{0,4},{4,0},{8,12},{12,8},{16,20},{20,16},{24,28},{28,24},{32,36},... | collective-permute-start | bytes 1572872 | tf_op jit(solution)/shard_map/ppermute | solution.py:234
  61.1 2.7 %project_near.2 = (bf16[128,2048]{1,0:T(8,128)(2,1)S(1)}, bf16[128,896]{1,0:T(8,128)(2,1)S(1)}) custom-call(bf16[128,2048]{1,0:T(8,128)(2,1)S(1)} %bitcast.20, f32[1,2048]{1,0:T(1,128)S(1)} %bitcast.21, bf16[2048,384]{1,0:T(8,128)(2,1)} %bitcast.31, bf16[2048,384]{1,0:T(8,128)(2,1)} %bitcast.34), custom_call_target="tpu_custom_call" | custom-call | flops 70848004096 | bytes 3145728 | tf_op jit(solution)/shard_map/project_near/pallas_call | solution.py:94
  63.8 8.1 %collective-permute-done.x_ref = bf16[128,2048]{1,0:T(8,128)(2,1)S(1)} collective-permute-done((bf16[128,2048]{1,0:T(8,128)(2,1)S(1)}, bf16[128,2048]{1,0:T(8,128)(2,1)S(1)}, u32[]{:S(2)}, u32[]{:S(2)}) %collective-permute-start) | collective-permute-done | bytes 524320 | tf_op jit(solution)/shard_map/ppermute | solution.py:234
  71.9 2.6 %project_near.3 = (bf16[128,2048]{1,0:T(8,128)(2,1)S(1)}, bf16[128,896]{1,0:T(8,128)(2,1)S(1)}) custom-call(bf16[128,2048]{1,0:T(8,128)(2,1)S(1)} %collective-permute-done.x_ref, f32[1,2048]{1,0:T(1,128)S(1)} %bitcast.22, bf16[2048,384]{1,0:T(8,128)(2,1)} %bitcast.32, bf16[2048,384]{1,0:T(8,128)(2,1)} %bitcast.35), custom_call_target="tpu_custom_call" | custom-call | flops 402653184 | bytes 3145728 | tf_op jit(solution)/shard_map/project_near/pallas_call | solution.py:94
  74.5 0.0 all-gather.3.cloned.1.call-done
  74.6 2.8 %project_far.2.mine_ref = bf16[128,1664]{1,0:T(8,128)(2,1)S(1)} custom-call(bf16[128,2048]{1,0:T(8,128)(2,1)S(1)} %get-tuple-element.17.scaled_ref, bf16[128,896]{1,0:T(8,128)(2,1)S(1)} %get-tuple-element.18.near_ref, bf16[8,3,256,384]{3,2,1,0:T(8,128)(2,1)} %bitcast.23), custom_call_target="tpu_custom_call" | custom-call | flops 402653184 | bytes 3145728 | tf_op jit(solution)/shard_map/project_far/pallas_call | solution.py:134
  77.4 3.3 %collective-permute-start.3 = (bf16[128,1664]{1,0:T(8,128)(2,1)S(1)}, bf16[128,1664]{1,0:T(8,128)(2,1)S(1)}, u32[]{:S(2)}, u32[]{:S(2)}) collective-permute-start(bf16[128,1664]{1,0:T(8,128)(2,1)S(1)} %project_far.2.mine_ref), channel_id=1, source_target_pairs={{0,1},{1,0},{2,3},{3,2},{4,5},{5,4},{6,7},{7,6},{8,9},{9,8},{10,11... | collective-permute-start | bytes 1277960 | tf_op jit(solution)/shard_map/ppermute | solution.py:242
  80.7 2.8 %project_far.3.mine_ref = bf16[128,1664]{1,0:T(8,128)(2,1)S(1)} custom-call(bf16[128,2048]{1,0:T(8,128)(2,1)S(1)} %get-tuple-element.13.scaled_ref, bf16[128,896]{1,0:T(8,128)(2,1)S(1)} %get-tuple-element.20.near_ref, bf16[8,3,256,384]{3,2,1,0:T(8,128)(2,1)} %bitcast.24), custom_call_target="tpu_custom_call" | custom-call | flops 402653184 | bytes 3145728 | tf_op jit(solution)/shard_map/project_far/pallas_call | solution.py:134
  83.5 2.5 %collective-permute-start.2 = (bf16[128,1664]{1,0:T(8,128)(2,1)S(1)}, bf16[128,1664]{1,0:T(8,128)(2,1)S(1)}, u32[]{:S(2)}, u32[]{:S(2)}) collective-permute-start(bf16[128,1664]{1,0:T(8,128)(2,1)S(1)} %project_far.3.mine_ref), channel_id=1, source_target_pairs={{0,1},{1,0},{2,3},{3,2},{4,5},{5,4},{6,7},{7,6},{8,9},{9,8},{10,11... | collective-permute-start | bytes 1277960 | tf_op jit(solution)/shard_map/ppermute | solution.py:245
  86.0 6.0 %collective-permute-done.3.sent_ref = bf16[128,1664]{1,0:T(8,128)(2,1)S(1)} collective-permute-done((bf16[128,1664]{1,0:T(8,128)(2,1)S(1)}, bf16[128,1664]{1,0:T(8,128)(2,1)S(1)}, u32[]{:S(2)}, u32[]{:S(2)}) %collective-permute-start.3) | collective-permute-done | bytes 426016 | tf_op jit(solution)/shard_map/ppermute | solution.py:242
  92.0 2.6 %expand.3 = bf16[128,2048]{1,0:T(8,128)(2,1)S(1)} custom-call(bf16[128,1664]{1,0:T(8,128)(2,1)S(1)} %project_far.2.mine_ref, bf16[128,1664]{1,0:T(8,128)(2,1)S(1)} %collective-permute-done.3.sent_ref, bf16[384,2048]{1,0:T(8,128)(2,1)} %bitcast.28, bf16[8,3,256,384]{3,2,1,0:T(8,128)(2,1)} %bitcast.25), custom_call_target="tpu_custom_call" | custom-call | flops 402653184 | bytes 3145728 | tf_op jit(solution)/shard_map/expand/pallas_call | solution.py:188
  94.7 2.9 %collective-permute-start.4 = (bf16[128,2048]{1,0:T(8,128)(2,1)S(1)}, bf16[128,2048]{1,0:T(8,128)(2,1)S(1)}, u32[]{:S(2)}, u32[]{:S(2)}) collective-permute-start(bf16[128,2048]{1,0:T(8,128)(2,1)S(1)} %expand.3), channel_id=1, source_target_pairs={{0,4},{4,0},{8,12},{12,8},{16,20},{20,16},{24,28},{28,24},{32,36},... | collective-permute-start | bytes 1572872 | tf_op jit(solution)/shard_map/ppermute | solution.py:248
  97.5 1.9 %collective-permute-done.2.sent_ref = bf16[128,1664]{1,0:T(8,128)(2,1)S(1)} collective-permute-done((bf16[128,1664]{1,0:T(8,128)(2,1)S(1)}, bf16[128,1664]{1,0:T(8,128)(2,1)S(1)}, u32[]{:S(2)}, u32[]{:S(2)}) %collective-permute-start.2) | collective-permute-done | bytes 426016 | tf_op jit(solution)/shard_map/ppermute | solution.py:245
  99.5 2.6 %expand.2 = f32[128,2048]{1,0:T(8,128)S(1)} custom-call(bf16[128,1664]{1,0:T(8,128)(2,1)S(1)} %project_far.3.mine_ref, bf16[128,1664]{1,0:T(8,128)(2,1)S(1)} %collective-permute-done.2.sent_ref, bf16[384,2048]{1,0:T(8,128)(2,1)} %bitcast.29, bf16[8,3,256,384]{3,2,1,0:T(8,128)(2,1)} %bitcast.26), custom_call_target="tpu_custom_call" | custom-call | flops 1107000064 | bytes 3145728 | tf_op jit(solution)/shard_map/expand/pallas_call | solution.py:188
  102.1 5.4 %collective-permute-done.4 = bf16[128,2048]{1,0:T(8,128)(2,1)S(1)} collective-permute-done((bf16[128,2048]{1,0:T(8,128)(2,1)S(1)}, bf16[128,2048]{1,0:T(8,128)(2,1)S(1)}, u32[]{:S(2)}, u32[]{:S(2)}) %collective-permute-start.4) | collective-permute-done | bytes 524320 | tf_op jit(solution)/shard_map/ppermute | solution.py:248
  107.5 0.9 add_convert_fusion
  108.4 12.0 %all-to-all-start.1 = ((bf16[8,16,2048]{2,1,0:T(8,128)(2,1)}), bf16[8,16,2048]{2,1,0:T(8,128)(2,1)S(1)}, u32[]{:S(2)}, u32[]{:S(2)}) async-start(bf16[8,16,2048]{2,1,0:T(8,128)(2,1)} %bitcast.12), calls=%async_computation.1 | async-start | bytes 1048576 | tf_op jit(solution)/shard_map/all_to_all | solution.py:249
  120.4 29.5 %all-to-all-done.1 = bf16[8,16,2048]{2,1,0:T(8,128)(2,1)S(1)} async-done(((bf16[8,16,2048]{2,1,0:T(8,128)(2,1)}), bf16[8,16,2048]{2,1,0:T(8,128)(2,1)S(1)}, u32[]{:S(2)}, u32[]{:S(2)}) %all-to-all-start.1) | async-done | bytes 524320 | tf_op jit(solution)/shard_map/all_to_all | solution.py:249
  149.9 0.2 fusion.3
  150.1 0.7 fusion.1
  (18 shorter events, 0.1 us)
Async XLA Ops:
  6.5 5.8 %copy-start = (bf16[32,2048]{1,0:T(8,128)(2,1)S(1)}, bf16[32,2048]{1,0:T(8,128)(2,1)}, u32[]{:S(2)}) copy-start(bf16[32,2048]{1,0:T(8,128)(2,1)} %param.7) | copy-start | bytes 393220
  6.5 5.3 %copy-start.3 = (s32[32,8]{0,1:T(8,128)S(1)}, s32[32,8]{0,1:T(8,128)}, u32[]{:S(2)}) copy-start(s32[32,8]{0,1:T(8,128)} %param.9) | copy-start | bytes 3076
  6.5 5.3 %copy-start.4 = (f32[32,8]{0,1:T(8,128)S(1)}, f32[32,8]{0,1:T(8,128)}, u32[]{:S(2)}) copy-start(f32[32,8]{0,1:T(8,128)} %param.10) | copy-start | bytes 3076
  7.7 53.4 %copy-start.1 = (f32[2048]{0:T(1024)S(1)}, f32[2048]{0:T(1024)}, u32[]{:S(2)}) copy-start(f32[2048]{0:T(1024)} %param.8) | copy-start | bytes 24580
  7.7 20.5 %collective-permute-start.1 = (bf16[3,256,384]{2,1,0:T(8,128)(2,1)S(1)}, bf16[3,256,384]{2,1,0:T(8,128)(2,1)S(1)}, u32[]{:S(2)}, u32[]{:S(2)}) collective-permute-start(bf16[3,256,384]{2,1,0:T(8,128)(2,1)S(1)} %share.1), channel_id=1, source_target_pairs={{0,2},{2,0},{1,3},{3,1},{4,6},{6,4},{5,7},{7,5},{8,10},{10,8},{9,1... | collective-permute-start | bytes 1769480 | tf_op jit(solution)/shard_map/ppermute | solution.py:215
  13.5 45.2 %all-to-all-start = ((bf16[8,16,2048]{2,1,0:T(8,128)(2,1)}), bf16[8,16,2048]{2,1,0:T(8,128)(2,1)S(1)}, u32[]{:S(2)}, u32[]{:S(2)}) async-start(bf16[8,16,2048]{2,1,0:T(8,128)(2,1)} %bitcast.4), calls=%async_computation | async-start | bytes 1048576 | tf_op jit(solution)/shard_map/all_to_all | solution.py:233
  28.1 46.4 %all-gather.3.cloned.1.call-start = ((), (), s32[]{:S(2)}) async-start(), calls=%async_computation.2 | async-start | bytes 5308416 | tf_op jit(solution)/shard_map/all_gather | solution.py:229
  28.2 0.8 copy-start.2
  58.7 13.2 %collective-permute-start = (bf16[128,2048]{1,0:T(8,128)(2,1)S(1)}, bf16[128,2048]{1,0:T(8,128)(2,1)S(1)}, u32[]{:S(2)}, u32[]{:S(2)}) collective-permute-start(bf16[128,2048]{1,0:T(8,128)(2,1)S(1)} %bitcast.19), channel_id=1, source_target_pairs={{0,4},{4,0},{8,12},{12,8},{16,20},{20,16},{24,28},{28,24},{32,36},... | collective-permute-start | bytes 1572872 | tf_op jit(solution)/shard_map/ppermute | solution.py:234
  77.4 14.6 %collective-permute-start.3 = (bf16[128,1664]{1,0:T(8,128)(2,1)S(1)}, bf16[128,1664]{1,0:T(8,128)(2,1)S(1)}, u32[]{:S(2)}, u32[]{:S(2)}) collective-permute-start(bf16[128,1664]{1,0:T(8,128)(2,1)S(1)} %project_far.2.mine_ref), channel_id=1, source_target_pairs={{0,1},{1,0},{2,3},{3,2},{4,5},{5,4},{6,7},{7,6},{8,9},{9,8},{10,11... | collective-permute-start | bytes 1277960 | tf_op jit(solution)/shard_map/ppermute | solution.py:242
  83.5 16.0 %collective-permute-start.2 = (bf16[128,1664]{1,0:T(8,128)(2,1)S(1)}, bf16[128,1664]{1,0:T(8,128)(2,1)S(1)}, u32[]{:S(2)}, u32[]{:S(2)}) collective-permute-start(bf16[128,1664]{1,0:T(8,128)(2,1)S(1)} %project_far.3.mine_ref), channel_id=1, source_target_pairs={{0,1},{1,0},{2,3},{3,2},{4,5},{5,4},{6,7},{7,6},{8,9},{9,8},{10,11... | collective-permute-start | bytes 1277960 | tf_op jit(solution)/shard_map/ppermute | solution.py:245
  94.7 12.8 %collective-permute-start.4 = (bf16[128,2048]{1,0:T(8,128)(2,1)S(1)}, bf16[128,2048]{1,0:T(8,128)(2,1)S(1)}, u32[]{:S(2)}, u32[]{:S(2)}) collective-permute-start(bf16[128,2048]{1,0:T(8,128)(2,1)S(1)} %expand.3), channel_id=1, source_target_pairs={{0,4},{4,0},{8,12},{12,8},{16,20},{20,16},{24,28},{28,24},{32,36},... | collective-permute-start | bytes 1572872 | tf_op jit(solution)/shard_map/ppermute | solution.py:248
  108.4 41.5 %all-to-all-start.1 = ((bf16[8,16,2048]{2,1,0:T(8,128)(2,1)}), bf16[8,16,2048]{2,1,0:T(8,128)(2,1)S(1)}, u32[]{:S(2)}, u32[]{:S(2)}) async-start(bf16[8,16,2048]{2,1,0:T(8,128)(2,1)} %bitcast.12), calls=%async_computation.1 | async-start | bytes 1048576 | tf_op jit(solution)/shard_map/all_to_all | solution.py:249
Sparse Core Ops, SparseCore 0:
  31.1 42.5 all-gather.2

commit v4 on v3

--- a/solution.py
+++ b/solution.py
@@ -106,47 +106,56 @@
     )(rows, gain, gate, up)
 
 
-def far_kernel(scaled_ref, near_ref, other_ref, send_ref, weights, sems):
+def far_kernel(first_ref, second_ref, near_ref, other_ref, first_send, early_send, late_send, weights, sems):
     pieces, _, depth, units = other_ref.shape
-    half, copies = pieces // 2, []
+    count, kept = near_ref.shape
+    half, part = pieces // 2, early_send.shape[0]
+    copies = []
     for piece in range(pieces):
         for i in range(2):
             rows = pl.ds(piece * depth, depth)
             copies.append(pltpu.make_async_copy(other_ref.at[piece, i], weights.at[i, rows], sems.at[piece, i]))
             copies[-1].start()
-    kept = near_ref.shape[1]
-    send_ref[:, :kept] = near_ref[...]
+    early_send[:, :kept] = near_ref[:part]
+    late_send[:, :kept] = near_ref[part:]
     totals = [None] * 2
     for step in range(2):
         for copy in copies[step * pieces : (step + 1) * pieces]:
             copy.wait()
         rows = slice(step * half * depth, (step + 1) * half * depth)
+        both = jnp.concatenate([second_ref[:, rows], first_ref[:, rows]])
         for i in range(2):
-            product = mm(scaled_ref[:, rows], weights[i, rows])
+            product = mm(both, weights[i, rows])
             totals[i] = product if step == 0 else totals[i] + product
     for i in range(2):
-        send_ref[:, kept + i * units : kept + (i + 1) * units] = totals[i].astype(jnp.bfloat16)
-
-
-def project_far(scaled, near_send, other):
-    (count, width), (pieces, _, _, units) = scaled.shape, other.shape
+        total = totals[i].astype(jnp.bfloat16)
+        at = slice(kept + i * units, kept + (i + 1) * units)
+        early_send[:, at] = total[:part]
+        late_send[:, at] = total[part:count]
+        first_send[:, i * units : (i + 1) * units] = total[count:]
+
+
+def project_far(first, second, near_send, other):
+    (count, width), (pieces, _, _, units) = first.shape, other.shape
     near, here = pl.BlockSpec(memory_space=pltpu.VMEM), pl.BlockSpec(memory_space=pltpu.HBM)
+    shape = (count // 2, near_send.shape[1] + 2 * units)
     return pl.pallas_call(
         far_kernel,
-        in_specs=[near] * 2 + [here],
-        out_specs=near,
-        out_shape=jax.ShapeDtypeStruct((count, near_send.shape[1] + 2 * units), jnp.bfloat16),
+        in_specs=[near] * 3 + [here],
+        out_specs=[near] * 3,
+        out_shape=[jax.ShapeDtypeStruct((count, 2 * units), jnp.bfloat16)]
+        + [jax.ShapeDtypeStruct(shape, jnp.bfloat16)] * 2,
         scratch_shapes=[pltpu.VMEM((2, width, units), jnp.bfloat16), pltpu.SemaphoreType.DMA((pieces, 2))],
         compiler_params=pltpu.CompilerParams(vmem_limit_bytes=VMEM_LIMIT),
         cost_estimate=pl.CostEstimate(
-            flops=4 * count * width * units, bytes_accessed=4 * width * units, transcendentals=0
+            flops=8 * count * width * units, bytes_accessed=4 * width * units, transcendentals=0
         ),
         name="project_far",
-    )(scaled, near_send, other)
-
-
-def expand_kernel(mine_ref, sent_ref, down_ref, other_ref, out_ref, down, hidden_ref, sems):
-    units, width = down_ref.shape
+    )(first, second, near_send, other)
+
+
+def expand_kernel(near_ref, near_sent_ref, far_ref, far_sent_ref, down_ref, other_ref, out_ref, down, hidden_ref, sems):
+    units = down_ref.shape[0]
     replicas, _, depth, _ = other_ref.shape
     rest = units - depth
     pairs = [(down_ref, down.at[pl.ds(0, units)])]
@@ -165,30 +174,32 @@
     for copy in copies:
         copy.start()
 
-    def both(at, size):
+    def both(mine, sent, at, size):
         at = pl.ds(at, size)
-        return mine_ref[:, at].astype(jnp.float32) + sent_ref[:, at].astype(jnp.float32)
-
-    total = jnp.sum(both(2 * units, LANES), axis=1, keepdims=True)
+        return mine[:, at].astype(jnp.float32) + sent[:, at].astype(jnp.float32)
+
+    total = jnp.sum(both(near_ref, near_sent_ref, 2 * units, LANES), axis=1, keepdims=True)
     scale = lax.rsqrt(total / D + EPSILON)
-    for piece in range(2):
-        at = piece * (2 * units + LANES)
-        gate, up = both(at, units), both(at + units, units)
+    kept = far_ref.shape[1] - 2 * units
+    for piece, (mine, sent, at) in enumerate(((near_ref, near_sent_ref, 0), (far_ref, far_sent_ref, kept))):
+        gate, up = both(mine, sent, at, units), both(mine, sent, at + units, units)
         hidden = jax.nn.silu(gate * scale) * (up * scale)
         hidden_ref[:, units * piece : units * (piece + 1)] = hidden.astype(jnp.bfloat16)
-    for copy in copies:
+    copies[0].wait()
+    out = mm(hidden_ref[:, :units], down[:units])
+    for copy in copies[1:]:
         copy.wait()
-    out_ref[...] = mm(hidden_ref[...], down[...]).astype(out_ref.dtype)
-
-
-def expand(mine, sent, down, other, kind, flops):
-    count, (units, width) = mine.shape[0], down.shape
-    near, here = pl.BlockSpec(memory_space=pltpu.VMEM), pl.BlockSpec(memory_space=pltpu.HBM)
+    out_ref[...] = (out + mm(hidden_ref[:, units:], down[units:])).astype(out_ref.dtype)
+
+
+def expand(near, near_sent, far, far_sent, down, other, kind, flops):
+    count, (units, width) = near.shape[0], down.shape
+    vmem, here = pl.BlockSpec(memory_space=pltpu.VMEM), pl.BlockSpec(memory_space=pltpu.HBM)
     replicas, _, depth, _ = other.shape
     return pl.pallas_call(
         expand_kernel,
-        in_specs=[near] * 2 + [here] * 2,
-        out_specs=near,
+        in_specs=[vmem] * 4 + [here] * 2,
+        out_specs=vmem,
         out_shape=jax.ShapeDtypeStruct((count, width), kind),
         scratch_shapes=[
             pltpu.VMEM((2 * units, width), jnp.bfloat16),
@@ -200,7 +211,7 @@
             flops=flops, bytes_accessed=4 * width * units, transcendentals=count * units
         ),
         name="expand",
-    )(mine, sent, down, other)
+    )(near, near_sent, far, far_sent, down, other)
 
 
 def shards(states, norm_gain, expert_ids, route_gates, w_gate, w_up, w_down):
@@ -236,16 +247,19 @@
     gain = norm_gain[None, :]
     gate, up = w_gate[0], w_up[0]
     scaled1, near1 = project_near(first, gain, gate, up, SCALE_FLOPS)
-    near1, second = lax.optimization_barrier((near1, second))
+    near_sent1 = lax.ppermute(near1, "xl", SWAP)
+    near_sent1, second = lax.optimization_barrier((near_sent1, second))
     scaled2, near2 = project_near(second, gain, gate, up, EXPAND_FLOPS)
-    send2 = project_far(scaled2, near2, other)
-    sent2 = lax.ppermute(send2, "xl", SWAP)
-    near1, _ = lax.optimization_barrier((near1, send2))
-    send1 = project_far(scaled1, near1, other)
-    sent1 = lax.ppermute(send1, "xl", SWAP)
-    out2 = expand(send2, sent2, w_down[0], other, jnp.bfloat16, EXPAND_FLOPS)
-    out1 = expand(send1, sent1, w_down[0], other, jnp.float32, WAIT_FLOPS)
-    out = (out1 + lax.ppermute(out2, "z", PAIRS).astype(jnp.float32)).astype(jnp.bfloat16)
+    far1, early, late = project_far(scaled1, scaled2, near2, other)
+    early_sent = lax.ppermute(early, "xl", SWAP)
+    late_sent = lax.ppermute(late, "xl", SWAP)
+    far_sent1 = lax.ppermute(far1, "xl", SWAP)
+    down = w_down[0]
+    outs = [expand(early, early_sent, early, early_sent, down, other, jnp.bfloat16, EXPAND_FLOPS)]
+    outs.append(expand(late, late_sent, late, late_sent, down, other, jnp.bfloat16, EXPAND_FLOPS))
+    out1 = expand(near1, near_sent1, far1, far_sent1, down, other, jnp.bfloat16, WAIT_FLOPS)
+    back = jnp.concatenate([lax.ppermute(x, "z", PAIRS) for x in outs])
+    out = (out1.astype(jnp.float32) + back.astype(jnp.float32)).astype(jnp.bfloat16)
     returned = exchange(out.reshape(experts, capacity, width)).reshape(rows, width)
 
     weighted = jnp.where(placed, jnp.repeat(weight.T, capacity, axis=0), 0.0)

time: 158 us -> 154 us (0.975)
  waiting for transfers between devices: 80.6 us -> 67.5 us
  starting transfers between devices: 41.8 us -> 50.1 us
    ppermute x3 -> x6, starting transfers between devices: 8.73 us -> 18.3 us  [the longest x2 5.84 us: shards(): back = jnp.concatenate([lax.ppermute(x, 'z', PAIRS) for x in outs])]
    ppermute x1, waiting for transfers between devices: 8.06 us -> 0.15 us  [shards(): second = lax.ppermute(first, 'z', PAIRS)]
    ppermute x3 -> x6, waiting for transfers between devices: 13.3 us -> 8.45 us  [the longest x1 4.6 us: shards(): near_sent1 = lax.ppermute(near1, 'xl', SWAP)]
  transfers between devices with their start and end apart: 8 -> 11, of which waited for: 6 -> 6; matrix products, arithmetic and copies ran while one was open for 1% -> 1% of each run, Pallas kernels for 8% -> 9%
where the time goes in v4:
time: 154 us
  waiting for transfers between devices  67.5 us (44%)
  starting transfers between devices  50.1 us (33%)
  Pallas kernels  18 us (12%)
  between operations  13.7 us (9%)
  other arithmetic  1.69 us (1%)
  matrix products  1.55 us (1%)
    all_to_all x1, waiting for transfers between devices, shards(): exchange(packed.reshape(experts, capacity, width)).reshape(rows, width)  29.7 us
    all_to_all x1, waiting for transfers between devices, shards(): exchange(out.reshape(experts, capacity, width)).reshape(rows, width)  29.1 us
    all_to_all x1, starting transfers between devices, shards(): exchange(packed.reshape(experts, capacity, width)).reshape(rows, width)  14.6 us
    all_to_all x1, starting transfers between devices, shards(): exchange(out.reshape(experts, capacity, width)).reshape(rows, width)  10.7 us
    pallas_call x3, Pallas kernels, expand(): pl.pallas_call(expand_kernel, in_specs=[vmem] * 4 + [here] * 2, out_specs...  8.18 us
    ppermute x2, starting transfers between devices, shards(): back = jnp.concatenate([lax.ppermute(x, 'z', PAIRS) for x in outs])  5.84 us
    pallas_call x2, Pallas kernels, project_near(): pl.pallas_call(near_kernel, in_specs=[near] * 2 + [here] * 2, out_specs=[...  5.32 us
    ppermute x1, waiting for transfers between devices, shards(): near_sent1 = lax.ppermute(near1, 'xl', SWAP)  4.6 us
  transfers between devices with their start and end apart: 11, of which 6 were waited for; matrix products, arithmetic and copies ran while one was open for 1% of the time, Pallas kernels for 9%

profile of v4, /device:TPU:2, one launch (start us, length us, event | category | flops | bytes accessed | tf_op | source)
XLA Modules:
  0.0 153.5 jit_solution(12767249959764044643)
XLA Ops:
  6.5 1.2 share.1
  7.7 4.0 %collective-permute-start.2 = (bf16[3,256,384]{2,1,0:T(8,128)(2,1)S(1)}, bf16[3,256,384]{2,1,0:T(8,128)(2,1)S(1)}, u32[]{:S(2)}, u32[]{:S(2)}) collective-permute-start(bf16[3,256,384]{2,1,0:T(8,128)(2,1)S(1)} %share.1), channel_id=1, source_target_pairs={{0,2},{2,0},{1,3},{3,1},{4,6},{6,4},{5,7},{7,5},{8,10},{10,8},{9,1... | collective-permute-start | bytes 1769480 | tf_op jit(solution)/shard_map/ppermute | solution.py:226
  11.9 0.1 eq.39
  11.9 0.1 copy.15
  12.0 0.2 fusion
  12.2 0.1 copy.14
  12.3 1.1 convolution_convert_fusion
  13.5 14.6 %all-to-all-start = ((bf16[8,16,2048]{2,1,0:T(8,128)(2,1)}), bf16[8,16,2048]{2,1,0:T(8,128)(2,1)S(1)}, u32[]{:S(2)}, u32[]{:S(2)}) async-start(bf16[8,16,2048]{2,1,0:T(8,128)(2,1)} %bitcast.4), calls=%async_computation | async-start | bytes 1048576 | tf_op jit(solution)/shard_map/all_to_all | solution.py:244
  28.2 0.8 copy-done.2
  29.0 29.7 %all-to-all-done = bf16[8,16,2048]{2,1,0:T(8,128)(2,1)S(1)} async-done(((bf16[8,16,2048]{2,1,0:T(8,128)(2,1)}), bf16[8,16,2048]{2,1,0:T(8,128)(2,1)S(1)}, u32[]{:S(2)}, u32[]{:S(2)}) %all-to-all-start) | async-done | bytes 524320 | tf_op jit(solution)/shard_map/all_to_all | solution.py:244
  58.7 2.4 %collective-permute-start.1 = (bf16[128,2048]{1,0:T(8,128)(2,1)S(1)}, bf16[128,2048]{1,0:T(8,128)(2,1)S(1)}, u32[]{:S(2)}, u32[]{:S(2)}) collective-permute-start(bf16[128,2048]{1,0:T(8,128)(2,1)S(1)} %bitcast.19), channel_id=1, source_target_pairs={{0,4},{4,0},{8,12},{12,8},{16,20},{20,16},{24,28},{28,24},{32,36},... | collective-permute-start | bytes 1572872 | tf_op jit(solution)/shard_map/ppermute | solution.py:245
  61.1 2.7 %project_near.2 = (bf16[128,2048]{1,0:T(8,128)(2,1)S(1)}, bf16[128,896]{1,0:T(8,128)(2,1)S(1)}) custom-call(bf16[128,2048]{1,0:T(8,128)(2,1)S(1)} %bitcast.20, f32[1,2048]{1,0:T(1,128)S(1)} %bitcast.21, bf16[2048,384]{1,0:T(8,128)(2,1)} %bitcast.32, bf16[2048,384]{1,0:T(8,128)(2,1)} %bitcast.35), custom_call_target="tpu_custom_call" | custom-call | flops 70848004096 | bytes 3145728 | tf_op jit(solution)/shard_map/project_near/pallas_call | solution.py:94
  63.8 3.3 %collective-permute-start = (bf16[128,896]{1,0:T(8,128)(2,1)S(1)}, bf16[128,896]{1,0:T(8,128)(2,1)S(1)}, u32[]{:S(2)}, u32[]{:S(2)}) collective-permute-start(bf16[128,896]{1,0:T(8,128)(2,1)S(1)} %get-tuple-element.15.near_ref), channel_id=1, source_target_pairs={{0,1},{1,0},{2,3},{3,2},{4,5},{5,4},{6,7},{7,6},{8,9},{9,8},{10,11... | collective-permute-start | bytes 688136 | tf_op jit(solution)/shard_map/ppermute | solution.py:250
  67.1 4.6 %collective-permute-done.near_sent_ref = bf16[128,896]{1,0:T(8,128)(2,1)S(1)} collective-permute-done((bf16[128,896]{1,0:T(8,128)(2,1)S(1)}, bf16[128,896]{1,0:T(8,128)(2,1)S(1)}, u32[]{:S(2)}, u32[]{:S(2)}) %collective-permute-start) | collective-permute-done | bytes 229408 | tf_op jit(solution)/shard_map/ppermute | solution.py:250
  71.7 0.1 collective-permute-done.1.x_ref
  71.9 2.6 %project_near.3 = (bf16[128,2048]{1,0:T(8,128)(2,1)S(1)}, bf16[128,896]{1,0:T(8,128)(2,1)S(1)}) custom-call(bf16[128,2048]{1,0:T(8,128)(2,1)S(1)} %collective-permute-done.1.x_ref, f32[1,2048]{1,0:T(1,128)S(1)} %bitcast.22, bf16[2048,384]{1,0:T(8,128)(2,1)} %bitcast.33, bf16[2048,384]{1,0:T(8,128)(2,1)} %bitcast.36), custom_call_target="tpu_custom_call" | custom-call | flops 402653184 | bytes 3145728 | tf_op jit(solution)/shard_map/project_near/pallas_call | solution.py:94
  74.5 3.3 %project_far.1 = (bf16[128,768]{1,0:T(8,128)(2,1)S(1)}, bf16[64,1664]{1,0:T(8,128)(2,1)S(1)}, bf16[64,1664]{1,0:T(8,128)(2,1)S(1)}) custom-call(bf16[128,2048]{1,0:T(8,128)(2,1)S(1)} %get-tuple-element.17.first_ref, bf16[128,2048]{1,0:T(8,128)(2,1)S(1)} %get-tuple-element.19.second_ref, bf16[128,896]{1,0:T(8,128)(2,1)S(1)} %get-tuple-element.20.near_ref, ...), custom_call_target="tpu_custom_call" | custom-call | flops 805306368 | bytes 3145728 | tf_op jit(solution)/shard_map/project_far/pallas_call | solution.py:142
  77.9 3.3 %collective-permute-start.6 = (bf16[64,1664]{1,0:T(8,128)(2,1)S(1)}, bf16[64,1664]{1,0:T(8,128)(2,1)S(1)}, u32[]{:S(2)}, u32[]{:S(2)}) collective-permute-start(bf16[64,1664]{1,0:T(8,128)(2,1)S(1)} %get-tuple-element.24.near_ref.far_ref), channel_id=1, source_target_pairs={{0,1},{1,0},{2,3},{3,2},{4,5},{5,4},{6,7},{7,6},{8,9},{9,8},{10,11... | collective-permute-start | bytes 638984 | tf_op jit(solution)/shard_map/ppermute | solution.py:255
  81.2 2.5 %collective-permute-start.4 = (bf16[64,1664]{1,0:T(8,128)(2,1)S(1)}, bf16[64,1664]{1,0:T(8,128)(2,1)S(1)}, u32[]{:S(2)}, u32[]{:S(2)}) collective-permute-start(bf16[64,1664]{1,0:T(8,128)(2,1)S(1)} %get-tuple-element.23.near_ref.far_ref), channel_id=1, source_target_pairs={{0,1},{1,0},{2,3},{3,2},{4,5},{5,4},{6,7},{7,6},{8,9},{9,8},{10,11... | collective-permute-start | bytes 638984 | tf_op jit(solution)/shard_map/ppermute | solution.py:254
  83.7 3.3 %collective-permute-start.3 = (bf16[128,768]{1,0:T(8,128)(2,1)S(1)}, bf16[128,768]{1,0:T(8,128)(2,1)S(1)}, u32[]{:S(2)}, u32[]{:S(2)}) collective-permute-start(bf16[128,768]{1,0:T(8,128)(2,1)S(1)} %get-tuple-element.22.far_ref), channel_id=1, source_target_pairs={{0,1},{1,0},{2,3},{3,2},{4,5},{5,4},{6,7},{7,6},{8,9},{9,8},{10,11... | collective-permute-start | bytes 589832 | tf_op jit(solution)/shard_map/ppermute | solution.py:256
  87.1 0.9 collective-permute-done.6.near_sent_ref.far_sent_ref
  88.0 2.7 %expand.5 = bf16[64,2048]{1,0:T(8,128)(2,1)S(1)} custom-call(bf16[64,1664]{1,0:T(8,128)(2,1)S(1)} %get-tuple-element.24.near_ref.far_ref, bf16[64,1664]{1,0:T(8,128)(2,1)S(1)} %collective-permute-done.6.near_sent_ref.far_sent_ref, bf16[64,1664]{1,0:T(8,128)(2,1)S(1)} %get-tuple-element.24.near_ref.far_ref, ...), custom_call_target="tpu_custom_call" | custom-call | flops 402653184 | bytes 3145728 | tf_op jit(solution)/shard_map/expand/pallas_call | solution.py:199
  90.7 3.3 %collective-permute-start.7 = (bf16[64,2048]{1,0:T(8,128)(2,1)S(1)}, bf16[64,2048]{1,0:T(8,128)(2,1)S(1)}, u32[]{:S(2)}, u32[]{:S(2)}) collective-permute-start(bf16[64,2048]{1,0:T(8,128)(2,1)S(1)} %expand.5), channel_id=1, source_target_pairs={{0,4},{4,0},{8,12},{12,8},{16,20},{20,16},{24,28},{28,24},{32,36},... | collective-permute-start | bytes 786440 | tf_op jit(solution)/shard_map/ppermute | solution.py:261
  94.0 2.7 %expand.4 = bf16[64,2048]{1,0:T(8,128)(2,1)S(1)} custom-call(bf16[64,1664]{1,0:T(8,128)(2,1)S(1)} %get-tuple-element.23.near_ref.far_ref, bf16[64,1664]{1,0:T(8,128)(2,1)S(1)} %collective-permute-done.4.near_sent_ref.far_sent_ref, bf16[64,1664]{1,0:T(8,128)(2,1)S(1)} %get-tuple-element.23.near_ref.far_ref, ...), custom_call_target="tpu_custom_call" | custom-call | flops 402653184 | bytes 3145728 | tf_op jit(solution)/shard_map/expand/pallas_call | solution.py:199
  96.7 2.6 %collective-permute-start.5 = (bf16[64,2048]{1,0:T(8,128)(2,1)S(1)}, bf16[64,2048]{1,0:T(8,128)(2,1)S(1)}, u32[]{:S(2)}, u32[]{:S(2)}) collective-permute-start(bf16[64,2048]{1,0:T(8,128)(2,1)S(1)} %expand.4), channel_id=1, source_target_pairs={{0,4},{4,0},{8,12},{12,8},{16,20},{20,16},{24,28},{28,24},{32,36},... | collective-permute-start | bytes 786440 | tf_op jit(solution)/shard_map/ppermute | solution.py:261
  99.3 2.8 %expand.3 = bf16[128,2048]{1,0:T(8,128)(2,1)S(1)} custom-call(bf16[128,896]{1,0:T(8,128)(2,1)S(1)} %get-tuple-element.15.near_ref, bf16[128,896]{1,0:T(8,128)(2,1)S(1)} %collective-permute-done.near_sent_ref, bf16[128,768]{1,0:T(8,128)(2,1)S(1)} %get-tuple-element.22.far_ref, bf16[128,768]{1,0:T(8,128)(2,1)S(1)} %collective-permute-done.3.far_sent_ref, ...), custom_call_target="tpu_custom_call" | custom-call | flops 1107000064 | bytes 3145728 | tf_op jit(solution)/shard_map/expand/pallas_call | solution.py:199
  102.1 2.9 %collective-permute-done.5 = bf16[64,2048]{1,0:T(8,128)(2,1)S(1)} collective-permute-done((bf16[64,2048]{1,0:T(8,128)(2,1)S(1)}, bf16[64,2048]{1,0:T(8,128)(2,1)S(1)}, u32[]{:S(2)}, u32[]{:S(2)}) %collective-permute-start.5) | collective-permute-done | bytes 262176 | tf_op jit(solution)/shard_map/ppermute | solution.py:261
  105.0 0.9 add_convert_fusion
  105.9 10.7 %all-to-all-start.1 = ((bf16[8,16,2048]{2,1,0:T(8,128)(2,1)}), bf16[8,16,2048]{2,1,0:T(8,128)(2,1)S(1)}, u32[]{:S(2)}, u32[]{:S(2)}) async-start(bf16[8,16,2048]{2,1,0:T(8,128)(2,1)} %bitcast.12), calls=%async_computation.1 | async-start | bytes 1048576 | tf_op jit(solution)/shard_map/all_to_all | solution.py:263
  116.6 29.1 %all-to-all-done.1 = bf16[8,16,2048]{2,1,0:T(8,128)(2,1)S(1)} async-done(((bf16[8,16,2048]{2,1,0:T(8,128)(2,1)}), bf16[8,16,2048]{2,1,0:T(8,128)(2,1)S(1)}, u32[]{:S(2)}, u32[]{:S(2)}) %all-to-all-start.1) | async-done | bytes 524320 | tf_op jit(solution)/shard_map/all_to_all | solution.py:263
  145.8 0.2 fusion.3
  146.0 0.7 fusion.1
  (24 shorter events, 0.2 us)
Async XLA Ops:
  6.5 5.8 %copy-start = (bf16[32,2048]{1,0:T(8,128)(2,1)S(1)}, bf16[32,2048]{1,0:T(8,128)(2,1)}, u32[]{:S(2)}) copy-start(bf16[32,2048]{1,0:T(8,128)(2,1)} %param.7) | copy-start | bytes 393220
  6.5 5.3 %copy-start.3 = (s32[32,8]{0,1:T(8,128)S(1)}, s32[32,8]{0,1:T(8,128)}, u32[]{:S(2)}) copy-start(s32[32,8]{0,1:T(8,128)} %param.9) | copy-start | bytes 3076
  6.5 5.3 %copy-start.4 = (f32[32,8]{0,1:T(8,128)S(1)}, f32[32,8]{0,1:T(8,128)}, u32[]{:S(2)}) copy-start(f32[32,8]{0,1:T(8,128)} %param.10) | copy-start | bytes 3076
  7.7 53.4 %copy-start.1 = (f32[2048]{0:T(1024)S(1)}, f32[2048]{0:T(1024)}, u32[]{:S(2)}) copy-start(f32[2048]{0:T(1024)} %param.8) | copy-start | bytes 24580
  7.7 20.4 %collective-permute-start.2 = (bf16[3,256,384]{2,1,0:T(8,128)(2,1)S(1)}, bf16[3,256,384]{2,1,0:T(8,128)(2,1)S(1)}, u32[]{:S(2)}, u32[]{:S(2)}) collective-permute-start(bf16[3,256,384]{2,1,0:T(8,128)(2,1)S(1)} %share.1), channel_id=1, source_target_pairs={{0,2},{2,0},{1,3},{3,1},{4,6},{6,4},{5,7},{7,5},{8,10},{10,8},{9,1... | collective-permute-start | bytes 1769480 | tf_op jit(solution)/shard_map/ppermute | solution.py:226
  13.5 45.2 %all-to-all-start = ((bf16[8,16,2048]{2,1,0:T(8,128)(2,1)}), bf16[8,16,2048]{2,1,0:T(8,128)(2,1)S(1)}, u32[]{:S(2)}, u32[]{:S(2)}) async-start(bf16[8,16,2048]{2,1,0:T(8,128)(2,1)} %bitcast.4), calls=%async_computation | async-start | bytes 1048576 | tf_op jit(solution)/shard_map/all_to_all | solution.py:244
  28.1 46.4 %all-gather.3.cloned.1.call-start = ((), (), s32[]{:S(2)}) async-start(), calls=%async_computation.2 | async-start | bytes 5308416 | tf_op jit(solution)/shard_map/all_gather | solution.py:240
  28.2 0.8 copy-start.2
  58.7 13.2 %collective-permute-start.1 = (bf16[128,2048]{1,0:T(8,128)(2,1)S(1)}, bf16[128,2048]{1,0:T(8,128)(2,1)S(1)}, u32[]{:S(2)}, u32[]{:S(2)}) collective-permute-start(bf16[128,2048]{1,0:T(8,128)(2,1)S(1)} %bitcast.19), channel_id=1, source_target_pairs={{0,4},{4,0},{8,12},{12,8},{16,20},{20,16},{24,28},{28,24},{32,36},... | collective-permute-start | bytes 1572872 | tf_op jit(solution)/shard_map/ppermute | solution.py:245
  63.8 7.9 %collective-permute-start = (bf16[128,896]{1,0:T(8,128)(2,1)S(1)}, bf16[128,896]{1,0:T(8,128)(2,1)S(1)}, u32[]{:S(2)}, u32[]{:S(2)}) collective-permute-start(bf16[128,896]{1,0:T(8,128)(2,1)S(1)} %get-tuple-element.15.near_ref), channel_id=1, source_target_pairs={{0,1},{1,0},{2,3},{3,2},{4,5},{5,4},{6,7},{7,6},{8,9},{9,8},{10,11... | collective-permute-start | bytes 688136 | tf_op jit(solution)/shard_map/ppermute | solution.py:250
  77.9 10.1 %collective-permute-start.6 = (bf16[64,1664]{1,0:T(8,128)(2,1)S(1)}, bf16[64,1664]{1,0:T(8,128)(2,1)S(1)}, u32[]{:S(2)}, u32[]{:S(2)}) collective-permute-start(bf16[64,1664]{1,0:T(8,128)(2,1)S(1)} %get-tuple-element.24.near_ref.far_ref), channel_id=1, source_target_pairs={{0,1},{1,0},{2,3},{3,2},{4,5},{5,4},{6,7},{7,6},{8,9},{9,8},{10,11... | collective-permute-start | bytes 638984 | tf_op jit(solution)/shard_map/ppermute | solution.py:255
  81.2 12.8 %collective-permute-start.4 = (bf16[64,1664]{1,0:T(8,128)(2,1)S(1)}, bf16[64,1664]{1,0:T(8,128)(2,1)S(1)}, u32[]{:S(2)}, u32[]{:S(2)}) collective-permute-start(bf16[64,1664]{1,0:T(8,128)(2,1)S(1)} %get-tuple-element.23.near_ref.far_ref), channel_id=1, source_target_pairs={{0,1},{1,0},{2,3},{3,2},{4,5},{5,4},{6,7},{7,6},{8,9},{9,8},{10,11... | collective-permute-start | bytes 638984 | tf_op jit(solution)/shard_map/ppermute | solution.py:254
  83.7 15.5 %collective-permute-start.3 = (bf16[128,768]{1,0:T(8,128)(2,1)S(1)}, bf16[128,768]{1,0:T(8,128)(2,1)S(1)}, u32[]{:S(2)}, u32[]{:S(2)}) collective-permute-start(bf16[128,768]{1,0:T(8,128)(2,1)S(1)} %get-tuple-element.22.far_ref), channel_id=1, source_target_pairs={{0,1},{1,0},{2,3},{3,2},{4,5},{5,4},{6,7},{7,6},{8,9},{9,8},{10,11... | collective-permute-start | bytes 589832 | tf_op jit(solution)/shard_map/ppermute | solution.py:256
  90.7 11.4 %collective-permute-start.7 = (bf16[64,2048]{1,0:T(8,128)(2,1)S(1)}, bf16[64,2048]{1,0:T(8,128)(2,1)S(1)}, u32[]{:S(2)}, u32[]{:S(2)}) collective-permute-start(bf16[64,2048]{1,0:T(8,128)(2,1)S(1)} %expand.5), channel_id=1, source_target_pairs={{0,4},{4,0},{8,12},{12,8},{16,20},{20,16},{24,28},{28,24},{32,36},... | collective-permute-start | bytes 786440 | tf_op jit(solution)/shard_map/ppermute | solution.py:261
  96.7 8.3 %collective-permute-start.5 = (bf16[64,2048]{1,0:T(8,128)(2,1)S(1)}, bf16[64,2048]{1,0:T(8,128)(2,1)S(1)}, u32[]{:S(2)}, u32[]{:S(2)}) collective-permute-start(bf16[64,2048]{1,0:T(8,128)(2,1)S(1)} %expand.4), channel_id=1, source_target_pairs={{0,4},{4,0},{8,12},{12,8},{16,20},{20,16},{24,28},{28,24},{32,36},... | collective-permute-start | bytes 786440 | tf_op jit(solution)/shard_map/ppermute | solution.py:261
  105.9 39.9 %all-to-all-start.1 = ((bf16[8,16,2048]{2,1,0:T(8,128)(2,1)}), bf16[8,16,2048]{2,1,0:T(8,128)(2,1)S(1)}, u32[]{:S(2)}, u32[]{:S(2)}) async-start(bf16[8,16,2048]{2,1,0:T(8,128)(2,1)} %bitcast.12), calls=%async_computation.1 | async-start | bytes 1048576 | tf_op jit(solution)/shard_map/all_to_all | solution.py:263
Sparse Core Ops, SparseCore 0:
  31.1 42.5 all-gather.2

commit v5 on v4

--- a/solution.py
+++ b/solution.py
@@ -13,14 +13,18 @@
 PAIRS = [(i, i ^ 1) for i in range(16)]
 LINES = [[0, 2, 4, 6, 9, 11, 13, 15], [1, 3, 5, 7, 8, 10, 12, 14]]
 LANES = 128
-VMEM_LIMIT = 52 * 1024 * 1024
+VMEM_LIMIT = 16 * 1024 * 1024
 EXPAND_FLOPS = 402653184
-WAIT_FLOPS = 1107000000
+WAIT_FLOPS = 1000000
 SCALE_FLOPS = 70848000000
 
 
 def mm(a, b):
     return jnp.dot(a, b, preferred_element_type=jnp.float32)
+
+
+def hbm(*arrays):
+    return [pltpu.with_memory_space_constraint(a, pltpu.HBM) for a in arrays]
 
 
 def share_kernel(replica, gate_ref, up_ref, down_ref, near_ref, sems):
@@ -56,7 +60,7 @@
         scratch_shapes=[pltpu.SemaphoreType.DMA((5,))],
         compiler_params=pltpu.CompilerParams(vmem_limit_bytes=VMEM_LIMIT),
         name="share",
-    )(replica, gate, up, down)
+    )(replica, *hbm(gate, up, down))
 
 
 def squares(values):
@@ -94,16 +98,45 @@
     return pl.pallas_call(
         near_kernel,
         in_specs=[near] * 2 + [here] * 2,
+        out_specs=[near] * 3,
+        out_shape=[
+            jax.ShapeDtypeStruct((count, width), jnp.bfloat16),
+            jax.ShapeDtypeStruct((count, 2 * units + LANES), jnp.bfloat16),
+            pltpu.VMEM((2, width, units), jnp.bfloat16),
+        ],
+        scratch_shapes=[pltpu.SemaphoreType.DMA((2, 2))],
+        compiler_params=pltpu.CompilerParams(vmem_limit_bytes=VMEM_LIMIT),
+        cost_estimate=pl.CostEstimate(flops=flops, bytes_accessed=4 * width * units, transcendentals=0),
+        name="project_near",
+    )(rows, gain, *hbm(gate, up))
+
+
+def again_kernel(x_ref, gain_ref, weights, scaled_ref, send_ref):
+    units = weights.shape[2]
+    values = x_ref[...].astype(jnp.float32)
+    send_ref[:, 2 * units :] = squares(values)
+    scaled_ref[...] = (values * gain_ref[...]).astype(jnp.bfloat16)
+    for i in range(2):
+        send_ref[:, i * units : (i + 1) * units] = mm(scaled_ref[...], weights[i]).astype(jnp.bfloat16)
+
+
+def project_again(rows, gain, weights):
+    (count, width), units = rows.shape, weights.shape[2]
+    near = pl.BlockSpec(memory_space=pltpu.VMEM)
+    return pl.pallas_call(
+        again_kernel,
+        in_specs=[near] * 3,
         out_specs=[near] * 2,
         out_shape=[
             jax.ShapeDtypeStruct((count, width), jnp.bfloat16),
             jax.ShapeDtypeStruct((count, 2 * units + LANES), jnp.bfloat16),
         ],
-        scratch_shapes=[pltpu.VMEM((2, width, units), jnp.bfloat16), pltpu.SemaphoreType.DMA((2, 2))],
-        compiler_params=pltpu.CompilerParams(vmem_limit_bytes=VMEM_LIMIT),
-        cost_estimate=pl.CostEstimate(flops=flops, bytes_accessed=4 * width * units, transcendentals=0),
-        name="project_near",
-    )(rows, gain, gate, up)
+        compiler_params=pltpu.CompilerParams(vmem_limit_bytes=VMEM_LIMIT),
+        cost_estimate=pl.CostEstimate(
+            flops=4 * count * width * units, bytes_accessed=4 * width * units, transcendentals=0
+        ),
+        name="project_again",
+    )(rows, gain, pltpu.with_memory_space_constraint(weights, pltpu.VMEM))
 
 
 def far_kernel(first_ref, second_ref, near_ref, other_ref, first_send, early_send, late_send, weights, sems):
@@ -145,34 +178,57 @@
         out_specs=[near] * 3,
         out_shape=[jax.ShapeDtypeStruct((count, 2 * units), jnp.bfloat16)]
         + [jax.ShapeDtypeStruct(shape, jnp.bfloat16)] * 2,
-        scratch_shapes=[pltpu.VMEM((2, width, units), jnp.bfloat16), pltpu.SemaphoreType.DMA((pieces, 2))],
+        scratch_shapes=[
+            pltpu.VMEM((2, width, units), jnp.bfloat16),
+            pltpu.SemaphoreType.DMA((pieces, 2)),
+        ],
         compiler_params=pltpu.CompilerParams(vmem_limit_bytes=VMEM_LIMIT),
         cost_estimate=pl.CostEstimate(
             flops=8 * count * width * units, bytes_accessed=4 * width * units, transcendentals=0
         ),
         name="project_far",
-    )(first, second, near_send, other)
-
-
-def expand_kernel(near_ref, near_sent_ref, far_ref, far_sent_ref, down_ref, other_ref, out_ref, down, hidden_ref, sems):
-    units = down_ref.shape[0]
-    replicas, _, depth, _ = other_ref.shape
+    )(first, second, near_send, *hbm(other))
+
+
+def stack_kernel(other_ref, down_ref, out_ref, sems):
+    pieces, _, depth, units = other_ref.shape
     rest = units - depth
-    pairs = [(down_ref, down.at[pl.ds(0, units)])]
-    for i in range(replicas):
+    pairs = [(down_ref, out_ref.at[pl.ds(0, units)])]
+    for i in range(pieces):
         pairs.append(
-            (other_ref.at[i, 2, :, pl.ds(0, depth)], down.at[pl.ds(units, depth), pl.ds(i * depth, depth)])
+            (other_ref.at[i, 2, :, pl.ds(0, depth)], out_ref.at[pl.ds(units, depth), pl.ds(i * depth, depth)])
         )
         for j in range(0, depth, rest):
             pairs.append(
                 (
                     other_ref.at[i, 2, pl.ds(j, rest), pl.ds(depth, rest)],
-                    down.at[pl.ds(units + depth, rest), pl.ds(i * depth + j, rest)],
+                    out_ref.at[pl.ds(units + depth, rest), pl.ds(i * depth + j, rest)],
                 )
             )
     copies = [pltpu.make_async_copy(a, b, sems.at[i]) for i, (a, b) in enumerate(pairs)]
     for copy in copies:
         copy.start()
+    for copy in copies:
+        copy.wait()
+
+
+def stack(other, down):
+    here = pl.BlockSpec(memory_space=pltpu.HBM)
+    (pieces, _, depth, units), width = other.shape, down.shape[1]
+    return pl.pallas_call(
+        stack_kernel,
+        in_specs=[here] * 2,
+        out_specs=pl.BlockSpec(memory_space=pltpu.VMEM),
+        out_shape=pltpu.VMEM((2 * units, width), jnp.bfloat16),
+        scratch_shapes=[pltpu.SemaphoreType.DMA((1 + pieces * (1 + depth // (units - depth)),))],
+        compiler_params=pltpu.CompilerParams(vmem_limit_bytes=VMEM_LIMIT),
+        cost_estimate=pl.CostEstimate(flops=0, bytes_accessed=8 * units * width, transcendentals=0),
+        name="stack",
+    )(*hbm(other, down))
+
+
+def expand_kernel(near_ref, near_sent_ref, far_ref, far_sent_ref, down_ref, out_ref, hidden_ref):
+    units = down_ref.shape[0] // 2
 
     def both(mine, sent, at, size):
         at = pl.ds(at, size)
@@ -185,33 +241,24 @@
         gate, up = both(mine, sent, at, units), both(mine, sent, at + units, units)
         hidden = jax.nn.silu(gate * scale) * (up * scale)
         hidden_ref[:, units * piece : units * (piece + 1)] = hidden.astype(jnp.bfloat16)
-    copies[0].wait()
-    out = mm(hidden_ref[:, :units], down[:units])
-    for copy in copies[1:]:
-        copy.wait()
-    out_ref[...] = (out + mm(hidden_ref[:, units:], down[units:])).astype(out_ref.dtype)
-
-
-def expand(near, near_sent, far, far_sent, down, other, kind, flops):
+    out_ref[...] = mm(hidden_ref[...], down_ref[...]).astype(out_ref.dtype)
+
+
+def expand(near, near_sent, far, far_sent, down, kind, flops):
     count, (units, width) = near.shape[0], down.shape
-    vmem, here = pl.BlockSpec(memory_space=pltpu.VMEM), pl.BlockSpec(memory_space=pltpu.HBM)
-    replicas, _, depth, _ = other.shape
+    vmem = pl.BlockSpec(memory_space=pltpu.VMEM)
     return pl.pallas_call(
         expand_kernel,
-        in_specs=[vmem] * 4 + [here] * 2,
+        in_specs=[vmem] * 5,
         out_specs=vmem,
         out_shape=jax.ShapeDtypeStruct((count, width), kind),
-        scratch_shapes=[
-            pltpu.VMEM((2 * units, width), jnp.bfloat16),
-            pltpu.VMEM((count, 2 * units), jnp.bfloat16),
-            pltpu.SemaphoreType.DMA((1 + replicas * (1 + depth // (units - depth)),)),
-        ],
+        scratch_shapes=[pltpu.VMEM((count, units), jnp.bfloat16)],
         compiler_params=pltpu.CompilerParams(vmem_limit_bytes=VMEM_LIMIT),
         cost_estimate=pl.CostEstimate(
-            flops=flops, bytes_accessed=4 * width * units, transcendentals=count * units
+            flops=flops, bytes_accessed=2 * width * units, transcendentals=count * units
         ),
         name="expand",
-    )(near, near_sent, far, far_sent, down, other)
+    )(near, near_sent, far, far_sent, pltpu.with_memory_space_constraint(down, pltpu.VMEM))
 
 
 def shards(states, norm_gain, expert_ids, route_gates, w_gate, w_up, w_down):
@@ -246,18 +293,20 @@
 
     gain = norm_gain[None, :]
     gate, up = w_gate[0], w_up[0]
-    scaled1, near1 = project_near(first, gain, gate, up, SCALE_FLOPS)
+    scaled1, near1, weights = project_near(first, gain, gate, up, SCALE_FLOPS)
     near_sent1 = lax.ppermute(near1, "xl", SWAP)
     near_sent1, second = lax.optimization_barrier((near_sent1, second))
-    scaled2, near2 = project_near(second, gain, gate, up, EXPAND_FLOPS)
+    scaled2, near2 = project_again(second, gain, weights)
     far1, early, late = project_far(scaled1, scaled2, near2, other)
     early_sent = lax.ppermute(early, "xl", SWAP)
     late_sent = lax.ppermute(late, "xl", SWAP)
+    other, _ = lax.optimization_barrier((other, early))
+    down = stack(other, w_down[0])
+    outs = [expand(early, early_sent, early, early_sent, down, jnp.bfloat16, EXPAND_FLOPS)]
+    far1, _ = lax.optimization_barrier((far1, outs[0]))
     far_sent1 = lax.ppermute(far1, "xl", SWAP)
-    down = w_down[0]
-    outs = [expand(early, early_sent, early, early_sent, down, other, jnp.bfloat16, EXPAND_FLOPS)]
-    outs.append(expand(late, late_sent, late, late_sent, down, other, jnp.bfloat16, EXPAND_FLOPS))
-    out1 = expand(near1, near_sent1, far1, far_sent1, down, other, jnp.bfloat16, WAIT_FLOPS)
+    outs.append(expand(late, late_sent, late, late_sent, down, jnp.bfloat16, EXPAND_FLOPS))
+    out1 = expand(near1, near_sent1, far1, far_sent1, down, jnp.bfloat16, WAIT_FLOPS)
     back = jnp.concatenate([lax.ppermute(x, "z", PAIRS) for x in outs])
     out = (out1.astype(jnp.float32) + back.astype(jnp.float32)).astype(jnp.bfloat16)
     returned = exchange(out.reshape(experts, capacity, width)).reshape(rows, width)

time: 154 us -> 153 us (level)
  Pallas kernels: 18 us -> 12.2 us
  waiting for transfers between devices: 67.5 us -> 71.5 us
    ppermute x1, waiting for transfers between devices: 0.01 us -> 5.38 us  [shards(): far_sent1 = lax.ppermute(far1, 'xl', SWAP)]
    pallas_call x3 -> x5, Pallas kernels: 8.18 us -> 4.95 us  [the longest x3 2.18 us: expand(): pl.pallas_call(expand_kernel, in_specs=[vmem] * 5, out_specs=vmem, out_sh...]
    ppermute x2, waiting for transfers between devices: 2.93 us -> 0.01 us  [shards(): back = jnp.concatenate([lax.ppermute(x, 'z', PAIRS) for x in outs])]
    pallas_call x2 -> x1, Pallas kernels: 5.32 us -> 2.72 us  [project_near(): pl.pallas_call(near_kernel, in_specs=[near] * 2 + [here] * 2, out_specs=[...]
  transfers between devices with their start and end apart: 11 -> 11, of which waited for: 6 -> 7; matrix products, arithmetic and copies ran while one was open for 1% -> 1% of each run, Pallas kernels for 9% -> 5%
where the time goes in v5:
time: 153 us; the launch traced here: 152 us
  waiting for transfers between devices  71.5 us (47%)
  starting transfers between devices  50.5 us (33%)
  between operations  13.6 us (9%)
  Pallas kernels  12.2 us (8%)
  other arithmetic  1.67 us (1%)
  matrix products  1.55 us (1%)
    all_to_all x1, waiting for transfers between devices, shards(): exchange(packed.reshape(experts, capacity, width)).reshape(rows, width)  29.7 us
    all_to_all x1, waiting for transfers between devices, shards(): exchange(out.reshape(experts, capacity, width)).reshape(rows, width)  28.6 us
    all_to_all x1, starting transfers between devices, shards(): exchange(packed.reshape(experts, capacity, width)).reshape(rows, width)  14.6 us
    all_to_all x1, starting transfers between devices, shards(): exchange(out.reshape(experts, capacity, width)).reshape(rows, width)  11.2 us
    ppermute x2, starting transfers between devices, shards(): back = jnp.concatenate([lax.ppermute(x, 'z', PAIRS) for x in outs])  6.59 us
    ppermute x1, waiting for transfers between devices, shards(): far_sent1 = lax.ppermute(far1, 'xl', SWAP)  5.38 us
    ppermute x1, waiting for transfers between devices, shards(): near_sent1 = lax.ppermute(near1, 'xl', SWAP)  4.61 us
    ppermute x1, starting transfers between devices, shards(): near = lax.ppermute(near, 'xh', SWAP)  4.03 us
  transfers between devices with their start and end apart: 11, of which 7 were waited for; matrix products, arithmetic and copies ran while one was open for 1% of the time, Pallas kernels for 5%

profile of v5, /device:TPU:2, one launch (start us, length us, event | category | flops | bytes accessed | tf_op | source)
XLA Modules:
  0.0 152.1 jit_solution(7141036585017259124)
XLA Ops:
  6.5 1.2 share.1
  7.7 4.0 %collective-permute-start.2 = (bf16[3,256,384]{2,1,0:T(8,128)(2,1)S(1)}, bf16[3,256,384]{2,1,0:T(8,128)(2,1)S(1)}, u32[]{:S(2)}, u32[]{:S(2)}) collective-permute-start(bf16[3,256,384]{2,1,0:T(8,128)(2,1)S(1)} %share.1), channel_id=1, source_target_pairs={{0,2},{2,0},{1,3},{3,1},{4,6},{6,4},{5,7},{7,5},{8,10},{10,8},{9,1... | collective-permute-start | bytes 1769480 | tf_op jit(solution)/shard_map/ppermute | solution.py:273
  11.9 0.2 fusion
  12.2 0.1 eq.39
  12.3 1.1 convolution_convert_fusion
  13.5 14.6 %all-to-all-start = ((bf16[8,16,2048]{2,1,0:T(8,128)(2,1)}), bf16[8,16,2048]{2,1,0:T(8,128)(2,1)S(1)}, u32[]{:S(2)}, u32[]{:S(2)}) async-start(bf16[8,16,2048]{2,1,0:T(8,128)(2,1)} %bitcast.4), calls=%async_computation | async-start | bytes 1048576 | tf_op jit(solution)/shard_map/all_to_all | solution.py:291
  28.2 0.8 copy-done.2
  29.0 29.7 %all-to-all-done = bf16[8,16,2048]{2,1,0:T(8,128)(2,1)S(1)} async-done(((bf16[8,16,2048]{2,1,0:T(8,128)(2,1)}), bf16[8,16,2048]{2,1,0:T(8,128)(2,1)S(1)}, u32[]{:S(2)}, u32[]{:S(2)}) %all-to-all-start) | async-done | bytes 524320 | tf_op jit(solution)/shard_map/all_to_all | solution.py:291
  58.7 2.4 %collective-permute-start.1 = (bf16[128,2048]{1,0:T(8,128)(2,1)S(1)}, bf16[128,2048]{1,0:T(8,128)(2,1)S(1)}, u32[]{:S(2)}, u32[]{:S(2)}) collective-permute-start(bf16[128,2048]{1,0:T(8,128)(2,1)S(1)} %bitcast.19), channel_id=1, source_target_pairs={{0,4},{4,0},{8,12},{12,8},{16,20},{20,16},{24,28},{28,24},{32,36},... | collective-permute-start | bytes 1572872 | tf_op jit(solution)/shard_map/ppermute | solution.py:292
  61.1 2.7 %project_near.1 = (bf16[128,2048]{1,0:T(8,128)(2,1)S(1)}, bf16[128,896]{1,0:T(8,128)(2,1)S(1)}, bf16[2,2048,384]{2,1,0:T(8,128)(2,1)S(1)}) custom-call(bf16[128,2048]{1,0:T(8,128)(2,1)S(1)} %bitcast.20, f32[1,2048]{1,0:T(1,128)S(1)} %bitcast.21, bf16[2048,384]{1,0:T(8,128)(2,1)} %bitcast.29, bf16[2048,384]{1,0:T(8,128)(2,1)} %bitcast.31), custom_call_target="tpu_custom_call" | custom-call | flops 70848004096 | bytes 3145728 | tf_op jit(solution)/shard_map/project_near/pallas_call | solution.py:98
  63.8 3.3 %collective-permute-start = (bf16[128,896]{1,0:T(8,128)(2,1)S(1)}, bf16[128,896]{1,0:T(8,128)(2,1)S(1)}, u32[]{:S(2)}, u32[]{:S(2)}) collective-permute-start(bf16[128,896]{1,0:T(8,128)(2,1)S(1)} %get-tuple-element.18.near_ref), channel_id=1, source_target_pairs={{0,1},{1,0},{2,3},{3,2},{4,5},{5,4},{6,7},{7,6},{8,9},{9,8},{10,11... | collective-permute-start | bytes 688136 | tf_op jit(solution)/shard_map/ppermute | solution.py:297
  67.1 4.6 %collective-permute-done.near_sent_ref = bf16[128,896]{1,0:T(8,128)(2,1)S(1)} collective-permute-done((bf16[128,896]{1,0:T(8,128)(2,1)S(1)}, bf16[128,896]{1,0:T(8,128)(2,1)S(1)}, u32[]{:S(2)}, u32[]{:S(2)}) %collective-permute-start) | collective-permute-done | bytes 229408 | tf_op jit(solution)/shard_map/ppermute | solution.py:297
  71.7 0.1 collective-permute-done.1.x_ref
  71.9 0.7 project_again.1
  72.6 1.0 all-gather.3.cloned.1.call-done
  73.6 3.3 %project_far.1 = (bf16[128,768]{1,0:T(8,128)(2,1)S(1)}, bf16[64,1664]{1,0:T(8,128)(2,1)S(1)}, bf16[64,1664]{1,0:T(8,128)(2,1)S(1)}) custom-call(bf16[128,2048]{1,0:T(8,128)(2,1)S(1)} %get-tuple-element.20.first_ref, bf16[128,2048]{1,0:T(8,128)(2,1)S(1)} %get-tuple-element.23.second_ref, bf16[128,896]{1,0:T(8,128)(2,1)S(1)} %get-tuple-element.24.near_ref, ...), custom_call_target="tpu_custom_call" | custom-call | flops 805306368 | bytes 3145728 | tf_op jit(solution)/shard_map/project_far/pallas_call | solution.py:175
  77.0 2.5 %collective-permute-start.6 = (bf16[64,1664]{1,0:T(8,128)(2,1)S(1)}, bf16[64,1664]{1,0:T(8,128)(2,1)S(1)}, u32[]{:S(2)}, u32[]{:S(2)}) collective-permute-start(bf16[64,1664]{1,0:T(8,128)(2,1)S(1)} %get-tuple-element.30.near_ref.far_ref), channel_id=1, source_target_pairs={{0,1},{1,0},{2,3},{3,2},{4,5},{5,4},{6,7},{7,6},{8,9},{9,8},{10,11... | collective-permute-start | bytes 638984 | tf_op jit(solution)/shard_map/ppermute | solution.py:302
  79.5 3.4 %collective-permute-start.3 = (bf16[64,1664]{1,0:T(8,128)(2,1)S(1)}, bf16[64,1664]{1,0:T(8,128)(2,1)S(1)}, u32[]{:S(2)}, u32[]{:S(2)}) collective-permute-start(bf16[64,1664]{1,0:T(8,128)(2,1)S(1)} %get-tuple-element.27.near_ref.far_ref), channel_id=1, source_target_pairs={{0,1},{1,0},{2,3},{3,2},{4,5},{5,4},{6,7},{7,6},{8,9},{9,8},{10,11... | collective-permute-start | bytes 638984 | tf_op jit(solution)/shard_map/ppermute | solution.py:301
  82.8 2.0 %stack.1.down_ref = bf16[768,2048]{1,0:T(8,128)(2,1)S(1)} custom-call(bf16[8,3,256,384]{3,2,1,0:T(8,128)(2,1)} %bitcast.24, bf16[384,2048]{1,0:T(8,128)(2,1)} %bitcast.26), custom_call_target="tpu_custom_call" | custom-call | bytes 6291456 | tf_op jit(solution)/shard_map/stack/pallas_call | solution.py:218
  84.9 2.1 %collective-permute-done.6.near_sent_ref.far_sent_ref = bf16[64,1664]{1,0:T(8,128)(2,1)S(1)} collective-permute-done((bf16[64,1664]{1,0:T(8,128)(2,1)S(1)}, bf16[64,1664]{1,0:T(8,128)(2,1)S(1)}, u32[]{:S(2)}, u32[]{:S(2)}) %collective-permute-start.6) | collective-permute-done | bytes 213024 | tf_op jit(solution)/shard_map/ppermute | solution.py:302
  87.0 0.7 expand.5
  87.7 3.5 %collective-permute-start.7 = (bf16[64,2048]{1,0:T(8,128)(2,1)S(1)}, bf16[64,2048]{1,0:T(8,128)(2,1)S(1)}, u32[]{:S(2)}, u32[]{:S(2)}) collective-permute-start(bf16[64,2048]{1,0:T(8,128)(2,1)S(1)} %expand.5), channel_id=1, source_target_pairs={{0,4},{4,0},{8,12},{12,8},{16,20},{20,16},{24,28},{28,24},{32,36},... | collective-permute-start | bytes 786440 | tf_op jit(solution)/shard_map/ppermute | solution.py:310
  91.2 0.7 expand.3
  91.9 3.1 %collective-permute-start.5 = (bf16[64,2048]{1,0:T(8,128)(2,1)S(1)}, bf16[64,2048]{1,0:T(8,128)(2,1)S(1)}, u32[]{:S(2)}, u32[]{:S(2)}) collective-permute-start(bf16[64,2048]{1,0:T(8,128)(2,1)S(1)} %expand.3), channel_id=1, source_target_pairs={{0,4},{4,0},{8,12},{12,8},{16,20},{20,16},{24,28},{28,24},{32,36},... | collective-permute-start | bytes 786440 | tf_op jit(solution)/shard_map/ppermute | solution.py:310
  95.1 2.5 %collective-permute-start.4 = (bf16[128,768]{1,0:T(8,128)(2,1)S(1)}, bf16[128,768]{1,0:T(8,128)(2,1)S(1)}, u32[]{:S(2)}, u32[]{:S(2)}) collective-permute-start(bf16[128,768]{1,0:T(8,128)(2,1)S(1)} %get-tuple-element.29.far_ref), channel_id=1, source_target_pairs={{0,1},{1,0},{2,3},{3,2},{4,5},{5,4},{6,7},{7,6},{8,9},{9,8},{10,11... | collective-permute-start | bytes 589832 | tf_op jit(solution)/shard_map/ppermute | solution.py:307
  97.5 5.4 %collective-permute-done.4.far_sent_ref = bf16[128,768]{1,0:T(8,128)(2,1)S(1)} collective-permute-done((bf16[128,768]{1,0:T(8,128)(2,1)S(1)}, bf16[128,768]{1,0:T(8,128)(2,1)S(1)}, u32[]{:S(2)}, u32[]{:S(2)}) %collective-permute-start.4) | collective-permute-done | bytes 196640 | tf_op jit(solution)/shard_map/ppermute | solution.py:307
  102.9 0.7 expand.4
  103.7 0.9 add_convert_fusion
  104.6 11.2 %all-to-all-start.1 = ((bf16[8,16,2048]{2,1,0:T(8,128)(2,1)}), bf16[8,16,2048]{2,1,0:T(8,128)(2,1)S(1)}, u32[]{:S(2)}, u32[]{:S(2)}) async-start(bf16[8,16,2048]{2,1,0:T(8,128)(2,1)} %bitcast.12), calls=%async_computation.1 | async-start | bytes 1048576 | tf_op jit(solution)/shard_map/all_to_all | solution.py:312
  115.8 28.6 %all-to-all-done.1 = bf16[8,16,2048]{2,1,0:T(8,128)(2,1)S(1)} async-done(((bf16[8,16,2048]{2,1,0:T(8,128)(2,1)}), bf16[8,16,2048]{2,1,0:T(8,128)(2,1)S(1)}, u32[]{:S(2)}, u32[]{:S(2)}) %all-to-all-start.1) | async-done | bytes 524320 | tf_op jit(solution)/shard_map/all_to_all | solution.py:312
  144.4 0.2 fusion.3
  144.6 0.7 fusion.1
  (25 shorter events, 0.3 us)
Async XLA Ops:
  6.5 5.8 %copy-start = (bf16[32,2048]{1,0:T(8,128)(2,1)S(1)}, bf16[32,2048]{1,0:T(8,128)(2,1)}, u32[]{:S(2)}) copy-start(bf16[32,2048]{1,0:T(8,128)(2,1)} %param.7) | copy-start | bytes 393220
  6.5 5.2 %copy-start.3 = (s32[32,8]{0,1:T(8,128)S(1)}, s32[32,8]{0,1:T(8,128)}, u32[]{:S(2)}) copy-start(s32[32,8]{0,1:T(8,128)} %param.9) | copy-start | bytes 3076
  6.5 5.3 %copy-start.4 = (f32[32,8]{0,1:T(8,128)S(1)}, f32[32,8]{0,1:T(8,128)}, u32[]{:S(2)}) copy-start(f32[32,8]{0,1:T(8,128)} %param.10) | copy-start | bytes 3076
  6.5 54.6 %copy-start.1 = (f32[2048]{0:T(1024)S(1)}, f32[2048]{0:T(1024)}, u32[]{:S(2)}) copy-start(f32[2048]{0:T(1024)} %param.8) | copy-start | bytes 24580
  7.7 20.4 %collective-permute-start.2 = (bf16[3,256,384]{2,1,0:T(8,128)(2,1)S(1)}, bf16[3,256,384]{2,1,0:T(8,128)(2,1)S(1)}, u32[]{:S(2)}, u32[]{:S(2)}) collective-permute-start(bf16[3,256,384]{2,1,0:T(8,128)(2,1)S(1)} %share.1), channel_id=1, source_target_pairs={{0,2},{2,0},{1,3},{3,1},{4,6},{6,4},{5,7},{7,5},{8,10},{10,8},{9,1... | collective-permute-start | bytes 1769480 | tf_op jit(solution)/shard_map/ppermute | solution.py:273
  13.5 45.2 %all-to-all-start = ((bf16[8,16,2048]{2,1,0:T(8,128)(2,1)}), bf16[8,16,2048]{2,1,0:T(8,128)(2,1)S(1)}, u32[]{:S(2)}, u32[]{:S(2)}) async-start(bf16[8,16,2048]{2,1,0:T(8,128)(2,1)} %bitcast.4), calls=%async_computation | async-start | bytes 1048576 | tf_op jit(solution)/shard_map/all_to_all | solution.py:291
  28.1 45.5 %all-gather.3.cloned.1.call-start = ((), (), s32[]{:S(2)}) async-start(), calls=%async_computation.2 | async-start | bytes 5308416 | tf_op jit(solution)/shard_map/all_gather | solution.py:287
  28.2 0.8 copy-start.2
  58.7 13.2 %collective-permute-start.1 = (bf16[128,2048]{1,0:T(8,128)(2,1)S(1)}, bf16[128,2048]{1,0:T(8,128)(2,1)S(1)}, u32[]{:S(2)}, u32[]{:S(2)}) collective-permute-start(bf16[128,2048]{1,0:T(8,128)(2,1)S(1)} %bitcast.19), channel_id=1, source_target_pairs={{0,4},{4,0},{8,12},{12,8},{16,20},{20,16},{24,28},{28,24},{32,36},... | collective-permute-start | bytes 1572872 | tf_op jit(solution)/shard_map/ppermute | solution.py:292
  63.8 7.9 %collective-permute-start = (bf16[128,896]{1,0:T(8,128)(2,1)S(1)}, bf16[128,896]{1,0:T(8,128)(2,1)S(1)}, u32[]{:S(2)}, u32[]{:S(2)}) collective-permute-start(bf16[128,896]{1,0:T(8,128)(2,1)S(1)} %get-tuple-element.18.near_ref), channel_id=1, source_target_pairs={{0,1},{1,0},{2,3},{3,2},{4,5},{5,4},{6,7},{7,6},{8,9},{9,8},{10,11... | collective-permute-start | bytes 688136 | tf_op jit(solution)/shard_map/ppermute | solution.py:297
  77.0 10.0 %collective-permute-start.6 = (bf16[64,1664]{1,0:T(8,128)(2,1)S(1)}, bf16[64,1664]{1,0:T(8,128)(2,1)S(1)}, u32[]{:S(2)}, u32[]{:S(2)}) collective-permute-start(bf16[64,1664]{1,0:T(8,128)(2,1)S(1)} %get-tuple-element.30.near_ref.far_ref), channel_id=1, source_target_pairs={{0,1},{1,0},{2,3},{3,2},{4,5},{5,4},{6,7},{7,6},{8,9},{9,8},{10,11... | collective-permute-start | bytes 638984 | tf_op jit(solution)/shard_map/ppermute | solution.py:302
  79.5 11.7 %collective-permute-start.3 = (bf16[64,1664]{1,0:T(8,128)(2,1)S(1)}, bf16[64,1664]{1,0:T(8,128)(2,1)S(1)}, u32[]{:S(2)}, u32[]{:S(2)}) collective-permute-start(bf16[64,1664]{1,0:T(8,128)(2,1)S(1)} %get-tuple-element.27.near_ref.far_ref), channel_id=1, source_target_pairs={{0,1},{1,0},{2,3},{3,2},{4,5},{5,4},{6,7},{7,6},{8,9},{9,8},{10,11... | collective-permute-start | bytes 638984 | tf_op jit(solution)/shard_map/ppermute | solution.py:301
  87.7 15.9 %collective-permute-start.7 = (bf16[64,2048]{1,0:T(8,128)(2,1)S(1)}, bf16[64,2048]{1,0:T(8,128)(2,1)S(1)}, u32[]{:S(2)}, u32[]{:S(2)}) collective-permute-start(bf16[64,2048]{1,0:T(8,128)(2,1)S(1)} %expand.5), channel_id=1, source_target_pairs={{0,4},{4,0},{8,12},{12,8},{16,20},{20,16},{24,28},{28,24},{32,36},... | collective-permute-start | bytes 786440 | tf_op jit(solution)/shard_map/ppermute | solution.py:310
  91.9 11.7 %collective-permute-start.5 = (bf16[64,2048]{1,0:T(8,128)(2,1)S(1)}, bf16[64,2048]{1,0:T(8,128)(2,1)S(1)}, u32[]{:S(2)}, u32[]{:S(2)}) collective-permute-start(bf16[64,2048]{1,0:T(8,128)(2,1)S(1)} %expand.3), channel_id=1, source_target_pairs={{0,4},{4,0},{8,12},{12,8},{16,20},{20,16},{24,28},{28,24},{32,36},... | collective-permute-start | bytes 786440 | tf_op jit(solution)/shard_map/ppermute | solution.py:310
  95.1 7.9 %collective-permute-start.4 = (bf16[128,768]{1,0:T(8,128)(2,1)S(1)}, bf16[128,768]{1,0:T(8,128)(2,1)S(1)}, u32[]{:S(2)}, u32[]{:S(2)}) collective-permute-start(bf16[128,768]{1,0:T(8,128)(2,1)S(1)} %get-tuple-element.29.far_ref), channel_id=1, source_target_pairs={{0,1},{1,0},{2,3},{3,2},{4,5},{5,4},{6,7},{7,6},{8,9},{9,8},{10,11... | collective-permute-start | bytes 589832 | tf_op jit(solution)/shard_map/ppermute | solution.py:307
  104.6 39.8 %all-to-all-start.1 = ((bf16[8,16,2048]{2,1,0:T(8,128)(2,1)}), bf16[8,16,2048]{2,1,0:T(8,128)(2,1)S(1)}, u32[]{:S(2)}, u32[]{:S(2)}) async-start(bf16[8,16,2048]{2,1,0:T(8,128)(2,1)} %bitcast.12), calls=%async_computation.1 | async-start | bytes 1048576 | tf_op jit(solution)/shard_map/all_to_all | solution.py:312
Sparse Core Ops, SparseCore 0:
  31.1 42.5 all-gather.2

commit v6 on v5

--- a/solution.py
+++ b/solution.py
@@ -61,6 +61,25 @@
         compiler_params=pltpu.CompilerParams(vmem_limit_bytes=VMEM_LIMIT),
         name="share",
     )(replica, *hbm(gate, up, down))
+
+
+def pack_kernel(placed_ref, states_ref, packed_ref):
+    packed_ref[...] = mm(placed_ref[...], states_ref[...]).astype(packed_ref.dtype)
+
+
+def pack(placed, states):
+    near = pl.BlockSpec(memory_space=pltpu.VMEM)
+    return pl.pallas_call(
+        pack_kernel,
+        in_specs=[near] * 2,
+        out_specs=near,
+        out_shape=pltpu.VMEM((placed.shape[0], states.shape[1]), jnp.bfloat16),
+        compiler_params=pltpu.CompilerParams(vmem_limit_bytes=VMEM_LIMIT),
+        cost_estimate=pl.CostEstimate(
+            flops=2 * placed.size * states.shape[1], bytes_accessed=8 * states.size, transcendentals=0
+        ),
+        name="pack",
+    )(placed, states)
 
 
 def squares(values):
@@ -282,7 +301,7 @@
     slot_ids = jnp.arange(capacity, dtype=jnp.int32)
     placed = slots.T[:, None, :] == slot_ids[None, :, None]
     placed = placed.reshape(rows, tokens)
-    packed = mm(placed.astype(jnp.bfloat16), states).astype(jnp.bfloat16)
+    packed = pack(placed.astype(jnp.bfloat16), states)
     near, _ = lax.optimization_barrier((near, packed))
     other = lax.all_gather(near, ("y", "core"), axis=0)
     exchange = functools.partial(

time: 153 us -> 153 us (level)
  transfers between devices with their start and end apart: 11 -> 11, of which waited for: 7 -> 7; matrix products, arithmetic and copies ran while one was open for 1% -> 0% of each run, Pallas kernels for 5% -> 6%
where the time goes in v6:
time: 153 us; the launch traced here: 152 us
  waiting for transfers between devices  71.5 us (47%)
  starting transfers between devices  50.3 us (33%)
  between operations  13.6 us (9%)
  Pallas kernels  13.2 us (9%)
  other arithmetic  1.9 us (1%)
    all_to_all x1, waiting for transfers between devices, shards(): exchange(packed.reshape(experts, capacity, width)).reshape(rows, width)  29.9 us
    all_to_all x1, waiting for transfers between devices, shards(): exchange(out.reshape(experts, capacity, width)).reshape(rows, width)  28.1 us
    all_to_all x1, starting transfers between devices, shards(): exchange(packed.reshape(experts, capacity, width)).reshape(rows, width)  14.7 us
    all_to_all x1, starting transfers between devices, shards(): exchange(out.reshape(experts, capacity, width)).reshape(rows, width)  11.2 us
    ppermute x2, starting transfers between devices, shards(): back = jnp.concatenate([lax.ppermute(x, 'z', PAIRS) for x in outs])  6.59 us
    ppermute x1, waiting for transfers between devices, shards(): far_sent1 = lax.ppermute(far1, 'xl', SWAP)  5.38 us
    ppermute x1, waiting for transfers between devices, shards(): near_sent1 = lax.ppermute(near1, 'xl', SWAP)  4.67 us
    ppermute x1, starting transfers between devices, shards(): near = lax.ppermute(near, 'xh', SWAP)  4.03 us
  transfers between devices with their start and end apart: 11, of which 7 were waited for; matrix products, arithmetic and copies ran while one was open for 0% of the time, Pallas kernels for 6%

profile of v6, /device:TPU:2, one launch (start us, length us, event | category | flops | bytes accessed | tf_op | source)
XLA Modules:
  0.0 152.0 jit_solution(13824587558102691623)
XLA Ops:
  6.5 1.2 share.1
  7.7 4.0 %collective-permute-start.2 = (bf16[3,256,384]{2,1,0:T(8,128)(2,1)S(1)}, bf16[3,256,384]{2,1,0:T(8,128)(2,1)S(1)}, u32[]{:S(2)}, u32[]{:S(2)}) collective-permute-start(bf16[3,256,384]{2,1,0:T(8,128)(2,1)S(1)} %share.1), channel_id=1, source_target_pairs={{0,2},{2,0},{1,3},{3,1},{4,6},{6,4},{5,7},{7,5},{8,10},{10,8},{9,1... | collective-permute-start | bytes 1769480 | tf_op jit(solution)/shard_map/ppermute | solution.py:292
  11.8 0.2 fusion
  12.1 0.1 fusion.5.placed_ref
  12.2 1.1 pack.1
  13.3 14.7 %all-to-all-start = ((bf16[8,16,2048]{2,1,0:T(8,128)(2,1)}), bf16[8,16,2048]{2,1,0:T(8,128)(2,1)S(1)}, u32[]{:S(2)}, u32[]{:S(2)}) async-start(bf16[8,16,2048]{2,1,0:T(8,128)(2,1)} %bitcast.4), calls=%async_computation | async-start | bytes 1048576 | tf_op jit(solution)/shard_map/all_to_all | solution.py:310
  28.0 0.8 copy-done.2
  28.8 29.9 %all-to-all-done = bf16[8,16,2048]{2,1,0:T(8,128)(2,1)S(1)} async-done(((bf16[8,16,2048]{2,1,0:T(8,128)(2,1)}), bf16[8,16,2048]{2,1,0:T(8,128)(2,1)S(1)}, u32[]{:S(2)}, u32[]{:S(2)}) %all-to-all-start) | async-done | bytes 524320 | tf_op jit(solution)/shard_map/all_to_all | solution.py:310
  58.7 2.2 %collective-permute-start.1 = (bf16[128,2048]{1,0:T(8,128)(2,1)S(1)}, bf16[128,2048]{1,0:T(8,128)(2,1)S(1)}, u32[]{:S(2)}, u32[]{:S(2)}) collective-permute-start(bf16[128,2048]{1,0:T(8,128)(2,1)S(1)} %bitcast.35), channel_id=1, source_target_pairs={{0,4},{4,0},{8,12},{12,8},{16,20},{20,16},{24,28},{28,24},{32,36},... | collective-permute-start | bytes 1572872 | tf_op jit(solution)/shard_map/ppermute | solution.py:311
  61.0 2.7 %project_near.1 = (bf16[128,2048]{1,0:T(8,128)(2,1)S(1)}, bf16[128,896]{1,0:T(8,128)(2,1)S(1)}, bf16[2,2048,384]{2,1,0:T(8,128)(2,1)S(1)}) custom-call(bf16[128,2048]{1,0:T(8,128)(2,1)S(1)} %bitcast.36, f32[1,2048]{1,0:T(1,128)S(1)} %bitcast.37, bf16[2048,384]{1,0:T(8,128)(2,1)} %bitcast.45, bf16[2048,384]{1,0:T(8,128)(2,1)} %bitcast.47), custom_call_target="tpu_custom_call" | custom-call | flops 70848004096 | bytes 3145728 | tf_op jit(solution)/shard_map/project_near/pallas_call | solution.py:117
  63.7 3.2 %collective-permute-start = (bf16[128,896]{1,0:T(8,128)(2,1)S(1)}, bf16[128,896]{1,0:T(8,128)(2,1)S(1)}, u32[]{:S(2)}, u32[]{:S(2)}) collective-permute-start(bf16[128,896]{1,0:T(8,128)(2,1)S(1)} %get-tuple-element.18.near_ref), channel_id=1, source_target_pairs={{0,1},{1,0},{2,3},{3,2},{4,5},{5,4},{6,7},{7,6},{8,9},{9,8},{10,11... | collective-permute-start | bytes 688136 | tf_op jit(solution)/shard_map/ppermute | solution.py:316
  66.9 4.7 %collective-permute-done.near_sent_ref = bf16[128,896]{1,0:T(8,128)(2,1)S(1)} collective-permute-done((bf16[128,896]{1,0:T(8,128)(2,1)S(1)}, bf16[128,896]{1,0:T(8,128)(2,1)S(1)}, u32[]{:S(2)}, u32[]{:S(2)}) %collective-permute-start) | collective-permute-done | bytes 229408 | tf_op jit(solution)/shard_map/ppermute | solution.py:316
  71.7 0.7 project_again.1
  72.4 1.2 all-gather.3.cloned.1.call-done
  73.6 3.3 %project_far.1 = (bf16[128,768]{1,0:T(8,128)(2,1)S(1)}, bf16[64,1664]{1,0:T(8,128)(2,1)S(1)}, bf16[64,1664]{1,0:T(8,128)(2,1)S(1)}) custom-call(bf16[128,2048]{1,0:T(8,128)(2,1)S(1)} %get-tuple-element.20.first_ref, bf16[128,2048]{1,0:T(8,128)(2,1)S(1)} %get-tuple-element.23.second_ref, bf16[128,896]{1,0:T(8,128)(2,1)S(1)} %get-tuple-element.24.near_ref, ...), custom_call_target="tpu_custom_call" | custom-call | flops 805306368 | bytes 3145728 | tf_op jit(solution)/shard_map/project_far/pallas_call | solution.py:194
  77.0 2.5 %collective-permute-start.6 = (bf16[64,1664]{1,0:T(8,128)(2,1)S(1)}, bf16[64,1664]{1,0:T(8,128)(2,1)S(1)}, u32[]{:S(2)}, u32[]{:S(2)}) collective-permute-start(bf16[64,1664]{1,0:T(8,128)(2,1)S(1)} %get-tuple-element.30.near_ref.far_ref), channel_id=1, source_target_pairs={{0,1},{1,0},{2,3},{3,2},{4,5},{5,4},{6,7},{7,6},{8,9},{9,8},{10,11... | collective-permute-start | bytes 638984 | tf_op jit(solution)/shard_map/ppermute | solution.py:321
  79.4 3.4 %collective-permute-start.3 = (bf16[64,1664]{1,0:T(8,128)(2,1)S(1)}, bf16[64,1664]{1,0:T(8,128)(2,1)S(1)}, u32[]{:S(2)}, u32[]{:S(2)}) collective-permute-start(bf16[64,1664]{1,0:T(8,128)(2,1)S(1)} %get-tuple-element.27.near_ref.far_ref), channel_id=1, source_target_pairs={{0,1},{1,0},{2,3},{3,2},{4,5},{5,4},{6,7},{7,6},{8,9},{9,8},{10,11... | collective-permute-start | bytes 638984 | tf_op jit(solution)/shard_map/ppermute | solution.py:320
  82.8 2.0 %stack.1.down_ref = bf16[768,2048]{1,0:T(8,128)(2,1)S(1)} custom-call(bf16[8,3,256,384]{3,2,1,0:T(8,128)(2,1)} %bitcast.40, bf16[384,2048]{1,0:T(8,128)(2,1)} %bitcast.42), custom_call_target="tpu_custom_call" | custom-call | bytes 6291456 | tf_op jit(solution)/shard_map/stack/pallas_call | solution.py:237
  84.9 2.1 %collective-permute-done.6.near_sent_ref.far_sent_ref = bf16[64,1664]{1,0:T(8,128)(2,1)S(1)} collective-permute-done((bf16[64,1664]{1,0:T(8,128)(2,1)S(1)}, bf16[64,1664]{1,0:T(8,128)(2,1)S(1)}, u32[]{:S(2)}, u32[]{:S(2)}) %collective-permute-start.6) | collective-permute-done | bytes 213024 | tf_op jit(solution)/shard_map/ppermute | solution.py:321
  86.9 0.7 expand.5
  87.7 3.5 %collective-permute-start.7 = (bf16[64,2048]{1,0:T(8,128)(2,1)S(1)}, bf16[64,2048]{1,0:T(8,128)(2,1)S(1)}, u32[]{:S(2)}, u32[]{:S(2)}) collective-permute-start(bf16[64,2048]{1,0:T(8,128)(2,1)S(1)} %expand.5), channel_id=1, source_target_pairs={{0,4},{4,0},{8,12},{12,8},{16,20},{20,16},{24,28},{28,24},{32,36},... | collective-permute-start | bytes 786440 | tf_op jit(solution)/shard_map/ppermute | solution.py:329
  91.2 0.7 expand.3
  91.9 3.1 %collective-permute-start.5 = (bf16[64,2048]{1,0:T(8,128)(2,1)S(1)}, bf16[64,2048]{1,0:T(8,128)(2,1)S(1)}, u32[]{:S(2)}, u32[]{:S(2)}) collective-permute-start(bf16[64,2048]{1,0:T(8,128)(2,1)S(1)} %expand.3), channel_id=1, source_target_pairs={{0,4},{4,0},{8,12},{12,8},{16,20},{20,16},{24,28},{28,24},{32,36},... | collective-permute-start | bytes 786440 | tf_op jit(solution)/shard_map/ppermute | solution.py:329
  95.1 2.5 %collective-permute-start.4 = (bf16[128,768]{1,0:T(8,128)(2,1)S(1)}, bf16[128,768]{1,0:T(8,128)(2,1)S(1)}, u32[]{:S(2)}, u32[]{:S(2)}) collective-permute-start(bf16[128,768]{1,0:T(8,128)(2,1)S(1)} %get-tuple-element.29.far_ref), channel_id=1, source_target_pairs={{0,1},{1,0},{2,3},{3,2},{4,5},{5,4},{6,7},{7,6},{8,9},{9,8},{10,11... | collective-permute-start | bytes 589832 | tf_op jit(solution)/shard_map/ppermute | solution.py:326
  97.5 5.4 %collective-permute-done.4.far_sent_ref = bf16[128,768]{1,0:T(8,128)(2,1)S(1)} collective-permute-done((bf16[128,768]{1,0:T(8,128)(2,1)S(1)}, bf16[128,768]{1,0:T(8,128)(2,1)S(1)}, u32[]{:S(2)}, u32[]{:S(2)}) %collective-permute-start.4) | collective-permute-done | bytes 196640 | tf_op jit(solution)/shard_map/ppermute | solution.py:326
  102.9 0.7 expand.4
  103.7 0.9 add_convert_fusion
  104.6 11.2 %all-to-all-start.1 = ((bf16[8,16,2048]{2,1,0:T(8,128)(2,1)}), bf16[8,16,2048]{2,1,0:T(8,128)(2,1)S(1)}, u32[]{:S(2)}, u32[]{:S(2)}) async-start(bf16[8,16,2048]{2,1,0:T(8,128)(2,1)} %bitcast.12), calls=%async_computation.1 | async-start | bytes 1048576 | tf_op jit(solution)/shard_map/all_to_all | solution.py:331
  115.9 0.1 fusion.4
  116.0 28.1 %all-to-all-done.1 = bf16[8,16,2048]{2,1,0:T(8,128)(2,1)S(1)} async-done(((bf16[8,16,2048]{2,1,0:T(8,128)(2,1)}), bf16[8,16,2048]{2,1,0:T(8,128)(2,1)S(1)}, u32[]{:S(2)}, u32[]{:S(2)}) %all-to-all-start.1) | async-done | bytes 524320 | tf_op jit(solution)/shard_map/all_to_all | solution.py:331
  144.1 0.3 fusion.6
  144.4 0.7 fusion.1
  (22 shorter events, 0.3 us)
Async XLA Ops:
  6.5 5.2 %copy-start.3 = (s32[32,8]{0,1:T(8,128)S(1)}, s32[32,8]{0,1:T(8,128)}, u32[]{:S(2)}) copy-start(s32[32,8]{0,1:T(8,128)} %param.9) | copy-start | bytes 3076
  6.5 5.6 %copy-start = (bf16[32,2048]{1,0:T(8,128)(2,1)S(1)}, bf16[32,2048]{1,0:T(8,128)(2,1)}, u32[]{:S(2)}) copy-start(bf16[32,2048]{1,0:T(8,128)(2,1)} %states_ref.1) | copy-start | bytes 393220
  6.5 54.4 %copy-start.1 = (f32[2048]{0:T(1024)S(1)}, f32[2048]{0:T(1024)}, u32[]{:S(2)}) copy-start(f32[2048]{0:T(1024)} %param.8) | copy-start | bytes 24580
  7.7 20.3 %collective-permute-start.2 = (bf16[3,256,384]{2,1,0:T(8,128)(2,1)S(1)}, bf16[3,256,384]{2,1,0:T(8,128)(2,1)S(1)}, u32[]{:S(2)}, u32[]{:S(2)}) collective-permute-start(bf16[3,256,384]{2,1,0:T(8,128)(2,1)S(1)} %share.1), channel_id=1, source_target_pairs={{0,2},{2,0},{1,3},{3,1},{4,6},{6,4},{5,7},{7,5},{8,10},{10,8},{9,1... | collective-permute-start | bytes 1769480 | tf_op jit(solution)/shard_map/ppermute | solution.py:292
  13.3 45.5 %all-to-all-start = ((bf16[8,16,2048]{2,1,0:T(8,128)(2,1)}), bf16[8,16,2048]{2,1,0:T(8,128)(2,1)S(1)}, u32[]{:S(2)}, u32[]{:S(2)}) async-start(bf16[8,16,2048]{2,1,0:T(8,128)(2,1)} %bitcast.4), calls=%async_computation | async-start | bytes 1048576 | tf_op jit(solution)/shard_map/all_to_all | solution.py:310
  27.9 45.7 %all-gather.3.cloned.1.call-start = ((), (), s32[]{:S(2)}) async-start(), calls=%async_computation.2 | async-start | bytes 5308416 | tf_op jit(solution)/shard_map/all_gather | solution.py:306
  28.0 0.8 copy-start.2
  58.7 12.9 %collective-permute-start.1 = (bf16[128,2048]{1,0:T(8,128)(2,1)S(1)}, bf16[128,2048]{1,0:T(8,128)(2,1)S(1)}, u32[]{:S(2)}, u32[]{:S(2)}) collective-permute-start(bf16[128,2048]{1,0:T(8,128)(2,1)S(1)} %bitcast.35), channel_id=1, source_target_pairs={{0,4},{4,0},{8,12},{12,8},{16,20},{20,16},{24,28},{28,24},{32,36},... | collective-permute-start | bytes 1572872 | tf_op jit(solution)/shard_map/ppermute | solution.py:311
  63.7 7.9 %collective-permute-start = (bf16[128,896]{1,0:T(8,128)(2,1)S(1)}, bf16[128,896]{1,0:T(8,128)(2,1)S(1)}, u32[]{:S(2)}, u32[]{:S(2)}) collective-permute-start(bf16[128,896]{1,0:T(8,128)(2,1)S(1)} %get-tuple-element.18.near_ref), channel_id=1, source_target_pairs={{0,1},{1,0},{2,3},{3,2},{4,5},{5,4},{6,7},{7,6},{8,9},{9,8},{10,11... | collective-permute-start | bytes 688136 | tf_op jit(solution)/shard_map/ppermute | solution.py:316
  77.0 10.0 %collective-permute-start.6 = (bf16[64,1664]{1,0:T(8,128)(2,1)S(1)}, bf16[64,1664]{1,0:T(8,128)(2,1)S(1)}, u32[]{:S(2)}, u32[]{:S(2)}) collective-permute-start(bf16[64,1664]{1,0:T(8,128)(2,1)S(1)} %get-tuple-element.30.near_ref.far_ref), channel_id=1, source_target_pairs={{0,1},{1,0},{2,3},{3,2},{4,5},{5,4},{6,7},{7,6},{8,9},{9,8},{10,11... | collective-permute-start | bytes 638984 | tf_op jit(solution)/shard_map/ppermute | solution.py:321
  79.4 11.7 %collective-permute-start.3 = (bf16[64,1664]{1,0:T(8,128)(2,1)S(1)}, bf16[64,1664]{1,0:T(8,128)(2,1)S(1)}, u32[]{:S(2)}, u32[]{:S(2)}) collective-permute-start(bf16[64,1664]{1,0:T(8,128)(2,1)S(1)} %get-tuple-element.27.near_ref.far_ref), channel_id=1, source_target_pairs={{0,1},{1,0},{2,3},{3,2},{4,5},{5,4},{6,7},{7,6},{8,9},{9,8},{10,11... | collective-permute-start | bytes 638984 | tf_op jit(solution)/shard_map/ppermute | solution.py:320
  87.7 15.9 %collective-permute-start.7 = (bf16[64,2048]{1,0:T(8,128)(2,1)S(1)}, bf16[64,2048]{1,0:T(8,128)(2,1)S(1)}, u32[]{:S(2)}, u32[]{:S(2)}) collective-permute-start(bf16[64,2048]{1,0:T(8,128)(2,1)S(1)} %expand.5), channel_id=1, source_target_pairs={{0,4},{4,0},{8,12},{12,8},{16,20},{20,16},{24,28},{28,24},{32,36},... | collective-permute-start | bytes 786440 | tf_op jit(solution)/shard_map/ppermute | solution.py:329
  91.9 11.7 %collective-permute-start.5 = (bf16[64,2048]{1,0:T(8,128)(2,1)S(1)}, bf16[64,2048]{1,0:T(8,128)(2,1)S(1)}, u32[]{:S(2)}, u32[]{:S(2)}) collective-permute-start(bf16[64,2048]{1,0:T(8,128)(2,1)S(1)} %expand.3), channel_id=1, source_target_pairs={{0,4},{4,0},{8,12},{12,8},{16,20},{20,16},{24,28},{28,24},{32,36},... | collective-permute-start | bytes 786440 | tf_op jit(solution)/shard_map/ppermute | solution.py:329
  95.1 20.7 %copy-start.4 = (f32[32,8]{0,1:T(8,128)S(1)}, f32[32,8]{0,1:T(8,128)}, u32[]{:S(2)}) copy-start(f32[32,8]{0,1:T(8,128)} %param.10) | copy-start | bytes 3076
  95.1 7.9 %collective-permute-start.4 = (bf16[128,768]{1,0:T(8,128)(2,1)S(1)}, bf16[128,768]{1,0:T(8,128)(2,1)S(1)}, u32[]{:S(2)}, u32[]{:S(2)}) collective-permute-start(bf16[128,768]{1,0:T(8,128)(2,1)S(1)} %get-tuple-element.29.far_ref), channel_id=1, source_target_pairs={{0,1},{1,0},{2,3},{3,2},{4,5},{5,4},{6,7},{7,6},{8,9},{9,8},{10,11... | collective-permute-start | bytes 589832 | tf_op jit(solution)/shard_map/ppermute | solution.py:326
  104.6 39.5 %all-to-all-start.1 = ((bf16[8,16,2048]{2,1,0:T(8,128)(2,1)}), bf16[8,16,2048]{2,1,0:T(8,128)(2,1)S(1)}, u32[]{:S(2)}, u32[]{:S(2)}) async-start(bf16[8,16,2048]{2,1,0:T(8,128)(2,1)} %bitcast.12), calls=%async_computation.1 | async-start | bytes 1048576 | tf_op jit(solution)/shard_map/all_to_all | solution.py:331
Sparse Core Ops, SparseCore 0:
  30.9 42.7 all-gather.2
